TPU v7x, 256 devices: a whole 4x4x8 slice. The times are simulated.
256 devices in a mesh: row: 16 (over y, z_lo, core), hid: 16 (over x, z_hi).
Axes of the slice: x: 4, y: 4, z: 8 (z_hi: 4, z_lo: 2; z = z_hi * 2 + z_lo), core: 2. Of those that a mesh axis runs over, the one named last changes fastest.
Arguments:
- inputs: bfloat16 [1024, 8192], P('hid', 'row'), may hold values from -6 to 6
- out_grad: bfloat16 [1024, 8192], P('hid', 'row'), may hold values from -2 to 2
- w_in: bfloat16 [8192, 32768], P('row', 'hid'), may hold values from -0.0625 to 0.0625
- w_out: bfloat16 [32768, 8192], P('hid', 'row'), may hold values from -0.03125 to 0.03125
Outputs:
- input_grad: float32 [1024, 8192], P('hid', 'row')
- w_in_grad: float32 [8192, 32768], P('row', 'hid')
- w_out_grad: float32 [32768, 8192], P('hid', 'row')
All inputs are finite; a program needn't handle non-finite values.
Results may differ from a plain program's by a relative error of at most 0.0029.
Values may be sent and summed in bfloat16 or wider, within the bound.
A program may use at most 128 MiB of HBM per device.

v0:
```python
import jax
import jax.numpy as jnp
from jax import lax
from jax.sharding import PartitionSpec as P


def gelu_parts(pre):
    phi = 0.5 * (1.0 + jax.scipy.special.erf(pre * 0.7071067811865476))
    dens = jnp.exp(-0.5 * pre * pre) * 0.3989422804014327
    return (pre * phi, phi + pre * dens)


def activate(pre, hidden_grad):
    value, slope = gelu_parts(pre)
    return (value.astype(jnp.bfloat16), (hidden_grad * slope).astype(jnp.bfloat16))


def local(inputs, out_grad, w_in, w_out):
    all_inputs, all_grads = (
        lax.all_gather(inputs, "hid", axis=0, tiled=True),
        lax.all_gather(out_grad, "hid", axis=0, tiled=True),
    )
    pre_part = jnp.dot(all_inputs, w_in, preferred_element_type=jnp.float32)
    hidden_part = lax.dot_general(
        all_grads, w_out, (((1,), (1,)), ((), ())), preferred_element_type=jnp.float32
    )
    pre_share, hidden_share = (
        lax.psum_scatter(pre_part, "row", scatter_dimension=0, tiled=True),
        lax.psum_scatter(hidden_part, "row", scatter_dimension=0, tiled=True),
    )
    act_share, grad_share = activate(pre_share, hidden_share)
    act, pre_grad = (
        lax.all_gather(act_share, "row", axis=0, tiled=True),
        lax.all_gather(grad_share, "row", axis=0, tiled=True),
    )
    w_out_grad = lax.dot_general(
        act, all_grads, (((0,), (0,)), ((), ())), preferred_element_type=jnp.float32
    )
    w_in_grad = lax.dot_general(
        all_inputs, pre_grad, (((0,), (0,)), ((), ())), preferred_element_type=jnp.float32
    )
    input_grad = lax.psum_scatter(
        lax.dot_general(
            pre_grad, w_in, (((1,), (1,)), ((), ())), preferred_element_type=jnp.float32
        ),
        "hid",
        scatter_dimension=0,
        tiled=True,
    )
    return (input_grad, w_in_grad, w_out_grad)


def solution(mesh):
    return jax.shard_map(
        local,
        mesh=mesh,
        in_specs=(P("hid", "row"), P("hid", "row"), P("row", "hid"), P("hid", "row")),
        out_specs=(P("hid", "row"), P("row", "hid"), P("hid", "row")),
        check_vma=False,
    )
```

profile of v0, /device:TPU:1, one launch (start us, length us, event | category | flops | bytes accessed | tf_op | source)
XLA Modules:
  0.0 502.8 jit_solution(12539987009937205984)
XLA Ops:
  7.2 0.0 copy-start
  7.2 0.0 all-gather.7.cloned.1.call-start
  7.2 0.7 all-gather.7.cloned.1.call-update
  7.9 0.0 all-gather.5.cloned.1.call-start
  8.0 0.7 all-gather.5.cloned.1.call-update
  8.7 0.0 reduce-scatter.6.cloned.1.call-start
  8.7 57.8 %all-gather.7.cloned.1.call-done = bf16[1024,512]{1,0:T(8,128)(2,1)} async-done(((bf16[64,512]{1,0:T(8,128)(2,1)}), bf16[1024,512]{1,0:T(8,128)(2,1)}) %all-gather.7.cloned.1.call-update) | async-done | bytes 1048592 | tf_op jit(solution)/shard_map/all_gather | solution.py:20
  66.5 0.0 copy-done
  66.5 6.8 %fusion.7 = f32[1024,2048]{1,0:T(8,128)} fusion(bf16[1024,512]{1,0:T(8,128)(2,1)} %all-gather.7.cloned.1.call-done, bf16[512,2048]{1,0:T(8,128)(2,1)S(1)} %copy-done), kind=kOutput, calls=%fused_computation.11 | convolution fusion | flops 2147483648 | bytes 11534336 | tf_op jit(solution)/shard_map/dot_general | solution.py:23
  73.3 0.0 reduce-scatter.6.cloned.1.call-update
  73.4 0.0 reduce-scatter.4.cloned.1.call-start
  73.4 46.3 %all-gather.5.cloned.1.call-done = bf16[1024,512]{1,0:T(8,128)(2,1)} async-done(((bf16[64,512]{1,0:T(8,128)(2,1)}), bf16[1024,512]{1,0:T(8,128)(2,1)}) %all-gather.5.cloned.1.call-update) | async-done | bytes 1048592 | tf_op jit(solution)/shard_map/all_gather | solution.py:21
  119.7 7.5 %fusion.6 = f32[1024,2048]{1,0:T(8,128)} fusion(bf16[1024,512]{1,0:T(8,128)(2,1)} %all-gather.5.cloned.1.call-done, bf16[2048,512]{1,0:T(8,128)(2,1)} %param.7), kind=kOutput, calls=%fused_computation.10 | convolution fusion | flops 2147483648 | bytes 11534336 | tf_op jit(solution)/shard_map/dot_general | solution.py:24
  127.3 0.0 reduce-scatter.4.cloned.1.call-update
  127.3 0.0 all-gather.9.cloned.1.call-start
  127.4 92.2 %reduce-scatter.6.cloned.1.call-done = f32[64,2048]{1,0:T(8,128)} async-done(((f32[1024,2048]{1,0:T(8,128)}), f32[64,2048]{1,0:T(8,128)}) %reduce-scatter.6.cloned.1.call-update) | async-done | bytes 524304 | tf_op jit(solution)/shard_map/reduce_scatter | solution.py:28
  219.6 101.3 %reduce-scatter.4.cloned.1.call-done = f32[64,2048]{1,0:T(8,128)} async-done(((f32[1024,2048]{1,0:T(8,128)}), f32[64,2048]{1,0:T(8,128)}) %reduce-scatter.4.cloned.1.call-update) | async-done | bytes 524304 | tf_op jit(solution)/shard_map/reduce_scatter | solution.py:29
  320.9 2.2 multiply_convert_fusion
  323.1 0.0 all-gather.9.cloned.1.call-update
  323.1 0.0 all-gather.11.cloned.1.call-start
  323.2 0.5 all-gather.11.cloned.1.call-update
  323.7 0.0 copy-start.2
  323.7 0.0 reduce-scatter.8.cloned.1.call-start
  323.7 40.0 %all-gather.9.cloned.1.call-done = bf16[1024,2048]{1,0:T(8,128)(2,1)} async-done(((bf16[64,2048]{1,0:T(8,128)(2,1)}), bf16[1024,2048]{1,0:T(8,128)(2,1)}) %all-gather.9.cloned.1.call-update) | async-done | bytes 4194320 | tf_op jit(solution)/shard_map/all_gather | solution.py:34
  363.8 5.9 %fusion.8 = f32[1024,512]{1,0:T(8,128)} fusion(bf16[1024,2048]{1,0:T(8,128)(2,1)} %all-gather.9.cloned.1.call-done, bf16[512,2048]{1,0:T(8,128)(2,1)S(1)} %copy-done), kind=kOutput, calls=%fused_computation.12 | convolution fusion | flops 2147483648 | bytes 8388608 | tf_op jit(solution)/shard_map/dot_general | solution.py:43
  369.7 0.0 reduce-scatter.8.cloned.1.call-update
  369.7 0.0 copy-done.2
  369.7 6.6 %convolution_bitcast_fusion = f32[512,2048]{0,1:T(8,128)} fusion(bf16[1024,2048]{1,0:T(8,128)(2,1)} %all-gather.9.cloned.1.call-done, bf16[1024,512]{1,0:T(8,128)(2,1)S(1)} %copy-done.2), kind=kOutput, calls=%fused_computation | convolution fusion | flops 2147483648 | bytes 9437184 | tf_op jit(solution)/shard_map/dot_general | solution.py:39
  376.3 0.0 copy-start.1
  376.3 5.6 %copy.7 = f32[512,2048]{1,0:T(8,128)} copy(f32[512,2048]{0,1:T(8,128)} %convolution_bitcast_fusion) | data formatting | bytes 8388608
  381.9 23.6 %all-gather.11.cloned.1.call-done = bf16[1024,2048]{1,0:T(8,128)(2,1)} async-done(((bf16[64,2048]{1,0:T(8,128)(2,1)}), bf16[1024,2048]{1,0:T(8,128)(2,1)}) %all-gather.11.cloned.1.call-update) | async-done | bytes 4194320 | tf_op jit(solution)/shard_map/all_gather | solution.py:33
  405.5 0.0 copy-done.1
  405.5 6.6 %fusion.9 = f32[2048,512]{1,0:T(8,128)} fusion(bf16[1024,2048]{1,0:T(8,128)(2,1)} %all-gather.11.cloned.1.call-done, bf16[1024,512]{1,0:T(8,128)(2,1)S(1)} %copy-done.1), kind=kOutput, calls=%fused_computation.13 | convolution fusion | flops 2147483648 | bytes 9437184 | tf_op jit(solution)/shard_map/dot_general | solution.py:36
  412.0 83.9 %reduce-scatter.8.cloned.1.call-done = f32[64,512]{1,0:T(8,128)} async-done(((f32[1024,512]{1,0:T(8,128)}), f32[64,512]{1,0:T(8,128)}) %reduce-scatter.8.cloned.1.call-update) | async-done | bytes 131088 | tf_op jit(solution)/shard_map/reduce_scatter | solution.py:42
Async XLA Ops:
  7.2 59.4 %copy-start = (bf16[512,2048]{1,0:T(8,128)(2,1)S(1)}, bf16[512,2048]{1,0:T(8,128)(2,1)}, u32[]{:S(2)}) copy-start(bf16[512,2048]{1,0:T(8,128)(2,1)} %param.6) | copy-start | bytes 6291460
  7.2 59.4 %all-gather.7.cloned.1.call-start = ((), (), s32[]{:S(2)}) async-start(), calls=%async_computation.5 | async-start | bytes 1114112 | tf_op jit(solution)/shard_map/all_gather | solution.py:20
  7.9 111.8 %all-gather.5.cloned.1.call-start = ((), (), s32[]{:S(2)}) async-start(), calls=%async_computation.3 | async-start | bytes 1114112 | tf_op jit(solution)/shard_map/all_gather | solution.py:21
  8.7 210.9 %reduce-scatter.6.cloned.1.call-start = ((), (), s32[]{:S(2)}) async-start(), calls=%async_computation.6 | async-start | bytes 8912896 | tf_op jit(solution)/shard_map/reduce_scatter | solution.py:28
  73.4 247.5 %reduce-scatter.4.cloned.1.call-start = ((), (), s32[]{:S(2)}) async-start(), calls=%async_computation.4 | async-start | bytes 8912896 | tf_op jit(solution)/shard_map/reduce_scatter | solution.py:29
  127.3 236.5 %all-gather.9.cloned.1.call-start = ((), (), s32[]{:S(2)}) async-start(), calls=%async_computation.7 | async-start | bytes 4456448 | tf_op jit(solution)/shard_map/all_gather | solution.py:34
  323.1 82.4 %all-gather.11.cloned.1.call-start = ((), (), s32[]{:S(2)}) async-start(), calls=%async_computation.9 | async-start | bytes 4456448 | tf_op jit(solution)/shard_map/all_gather | solution.py:33
  323.7 46.0 %copy-start.2 = (bf16[1024,512]{1,0:T(8,128)(2,1)S(1)}, bf16[1024,512]{1,0:T(8,128)(2,1)}, u32[]{:S(2)}) copy-start(bf16[1024,512]{1,0:T(8,128)(2,1)} %all-gather.7.cloned.1.call-done) | copy-start | bytes 3145732
  323.7 172.3 %reduce-scatter.8.cloned.1.call-start = ((), (), s32[]{:S(2)}) async-start(), calls=%async_computation.8 | async-start | bytes 2228224 | tf_op jit(solution)/shard_map/reduce_scatter | solution.py:42
  376.3 29.2 %copy-start.1 = (bf16[1024,512]{1,0:T(8,128)(2,1)S(1)}, bf16[1024,512]{1,0:T(8,128)(2,1)}, u32[]{:S(2)}) copy-start(bf16[1024,512]{1,0:T(8,128)(2,1)} %all-gather.5.cloned.1.call-done) | copy-start | bytes 3145732
Sparse Core Ops, SparseCore 0:
  10.4 56.0 all-gather.6
  69.0 50.7 all-gather.4
  122.3 97.2 reduce-scatter.5
  222.0 98.8 reduce-scatter.3
  323.2 40.4 all-gather.8
  365.5 39.9 all-gather.10
  409.6 86.3 reduce-scatter.7
where the time goes:
time: 504 us; the launch traced here: 503 us
  waiting for transfers between devices  447 us (89%)
  matrix products  33.4 us (7%)
  between operations  14.2 us (3%)
  local copies, waits for them, and re-layouts  5.58 us (1%)
    reduce_scatter x1, waiting for transfers between devices, local(): lax.psum_scatter(hidden_part, 'row', scatter_dimension=0, tiled=True)  101 us
    reduce_scatter x1, waiting for transfers between devices, local(): lax.psum_scatter(pre_part, 'row', scatter_dimension=0, tiled=True)  92.2 us
    reduce_scatter x1, waiting for transfers between devices, local(): lax.psum_scatter(lax.dot_general(pre_grad, w_in, (((1,), (1,)), ((), ()))...  83.9 us
    all_gather x1, waiting for transfers between devices, local(): lax.all_gather(inputs, 'hid', axis=0, tiled=True)  57.8 us
    all_gather x1, waiting for transfers between devices, local(): lax.all_gather(out_grad, 'hid', axis=0, tiled=True)  46.3 us
    all_gather x1, waiting for transfers between devices, local(): lax.all_gather(grad_share, 'row', axis=0, tiled=True)  40 us
    all_gather x1, waiting for transfers between devices, local(): lax.all_gather(act_share, 'row', axis=0, tiled=True)  23.6 us
  transfers between devices with their start and end apart: 7, of which 7 were waited for; matrix products, arithmetic and copies ran while one was open for 8% of the time, Pallas kernels for 0%

commit v1 on v0

v1 whole, which is shorter than its diff:
```python
import functools

import jax
import jax.numpy as jnp
from jax import lax
from jax.experimental import pallas as pl
from jax.experimental.pallas import tpu as pltpu
from jax.sharding import PartitionSpec as P

MESH = pl.DeviceIdType.MESH
F32 = jnp.float32
BF16 = jnp.bfloat16
NC = 4
NT = (((1,), (1,)), ((), ()))

STAGES = {
    "A": (0, 6), "B": (5, 7), "C": (9, 9), "D": (12, 13), "E": (14, 16), "F": (19, 16), "G": (23.5, 16),
    "H": (27.5, 16), "I": (31.5, 16), "J": (38, 16), "K": (42, 16), "L": (45, 16), "M": (48, 16),
    "N": (51, 16), "O": (54, 16),
}
COPIES = [
    "A1", "A2", "A3", "B0", "B1", "C0", "C1", "D",
    "y00", "y01", "y02", "y10", "y11", "y12", "z", "H", "I0", "I1", "J0", "J1", "K",
    "x00", "x01", "x02", "x10", "x11", "x12", "N1", "N2", "N3",
]
NSEM = len(COPIES) * NC + 2


def gelu_parts(pre):
    phi = 0.5 * (1.0 + lax.erf(pre * 0.7071067811865476))
    dens = jnp.exp(-0.5 * pre * pre) * 0.3989422804014327
    return (pre * phi, phi + pre * dens)


UP, DOWN = 2.0**50, 2.0**-50


def encode(v):
    return ((v * UP) * (jnp.abs(v) * UP)).astype(BF16)


def decode(q):
    q = q.astype(F32)
    root = jnp.sqrt(jnp.abs(q)) * DOWN
    return jnp.where(q < 0, -root, root)


def kernel(x_ref, g_ref, w_in, w_out, ig_ref, xo, ao,
           XG, W1, W2, PT, TX, RX, ZT, ZR, ACT, IGP, XR, ZX, ssem, rsem, lsem, wsem):
    r, h = lax.axis_index("row"), lax.axis_index("hid")
    core, zl, y = r % 2, (r // 2) % 2, r // 4
    x, zh = h // 4, h % 4

    def dev(y=y, zl=zl, core=core, x=x, zh=zh):
        return {"row": (y * 2 + zl) * 2 + core, "hid": x * 4 + zh}

    yr, yl, yf = (y + 1) % 4, (y + 3) % 4, (y + 2) % 4
    xr, xl, xf = (x + 1) % 4, (x + 3) % 4, (x + 2) % 4
    right, left = dev(y=yr), dev(y=yl)
    xright, xleft = dev(x=xr), dev(x=xl)
    partner, zpair = dev(core=1 - core), dev(zl=1 - zl)
    zmate = {j: dev(zh=(zh + j) % 4) for j in (1, 2, 3)}

    barrier = pltpu.get_barrier_semaphore()
    others = [right, left, xright, xleft, partner, zpair, zmate[1], zmate[2], zmate[3]]
    for other in others:
        pl.semaphore_signal(barrier, inc=1, device_id=other, device_id_type=MESH)
    pl.semaphore_wait(barrier, len(others))

    copies = {}
    locals_ = []

    def send(name, c, src, dst, to):
        i = COPIES.index(name) + len(COPIES) * c if c is not None else NSEM - 2 + name
        copy = pltpu.make_async_remote_copy(
            src_ref=src, dst_ref=dst, send_sem=ssem.at[i], recv_sem=rsem.at[i], device_id=to, device_id_type=MESH
        )
        copy.start()
        copies[name, c] = copy

    def arrived(c, *names):
        for name in names:
            copies[name, c].wait_recv()

    def keep(src, dst):
        copy = pltpu.make_async_copy(src, dst, lsem.at[len(locals_)])
        copy.start()
        locals_.append(copy)

    def A(c):
        rows = pl.ds(16 * c, 16)
        XG[c, 0, core, h] = x_ref[rows, :]
        XG[c, 1, core, h] = g_ref[rows, :]
        mine = XG.at[c, :, core, h]
        for j in (1, 2, 3):
            send(f"A{j}", c, mine, mine, zmate[j])

    def B(c):
        arrived(c, "A1", "A2", "A3")
        mine = XG.at[c, :, core, pl.ds(4 * x, 4)]
        send("B0", c, mine, mine, xright)
        send("B1", c, mine, mine, xleft)

    def C(c):
        arrived(c, "B0")
        block = XG.at[c, :, core, pl.ds(4 * xl, 2)]
        send("C0", c, block, block, xright)
        arrived(c, "B1")
        block = XG.at[c, :, core, pl.ds(4 * xr + 2, 2)]
        send("C1", c, block, block, xleft)

    def D(c):
        arrived(c, "C0", "C1")
        mine = XG.at[c, :, core]
        send("D", c, mine, mine, partner)
        for a in range(2):
            keep(XG.at[c, a, core], xo.at[a, c])

    def E(c):
        if c == 0:
            copies[0, None].wait_recv()
            copies[1, None].wait_recv()
            for copy in own:
                copy.wait()
        arrived(c, "D")

        @pl.loop(0, 4)
        def _(n):
            cols = pl.ds(pl.multiple_of(n * 256, 256), 256)
            pre = jnp.dot(XG[c, 0, 0].reshape(256, 512), W1[0, :, cols], preferred_element_type=F32)
            pre += jnp.dot(XG[c, 0, 1].reshape(256, 512), W1[1, :, cols], preferred_element_type=F32)
            PT[c, 0, :, :, :, cols] = pre.reshape(4, 2, 32, 256)
            hid = lax.dot_general(XG[c, 1, 0].reshape(256, 512), W2[0, cols, :], NT, preferred_element_type=F32)
            hid += lax.dot_general(XG[c, 1, 1].reshape(256, 512), W2[1, cols, :], NT, preferred_element_type=F32)
            PT[c, 1, :, :, :, cols] = hid.reshape(4, 2, 32, 256)

        for d, kind, piece, half, to in (
            (0, 0, yf, 0, right), (1, 0, yf, 1, left), (0, 1, yr, 1, right), (1, 1, yl, 0, left),
        ):
            for a in range(2):
                TX[c, d, kind, a] = encode(PT[c, a, piece, half])
            send(f"y{d}{kind}", c, TX.at[c, d, kind], RX.at[c, d, kind], to)

    def F(c):
        for d, piece, half, to in ((0, yr, 0, right), (1, yl, 1, left)):
            arrived(c, f"y{d}0")
            for a in range(2):
                TX[c, d, 2, a] = encode(PT[c, a, piece, half] + decode(RX[c, d, 0, a]))
            send(f"y{d}2", c, TX.at[c, d, 2], RX.at[c, d, 2], to)

    def G(c):
        arrived(c, "y01", "y11", "y02", "y12")
        for half in (1 - zl, zl):
            for a in range(2):
                total = PT[c, a, y, half] + decode(RX[c, 0, 2 - half, a]) + decode(RX[c, 1, 1 + half, a])
                if half is zl:
                    PT[c, a, y, half] = total
                else:
                    ZT[c, a] = encode(total)
            if half is not zl:
                send("z", c, ZT.at[c], ZR.at[c], zpair)

    def H(c):
        arrived(c, "z")
        pre = PT[c, 0, y, zl] + decode(ZR[c, 0])
        hidden = PT[c, 1, y, zl] + decode(ZR[c, 1])
        value, slope = gelu_parts(pre)
        ACT[c, 0, core, y, zl] = value.astype(BF16)
        ACT[c, 1, core, y, zl] = (hidden * slope).astype(BF16)
        mine = ACT.at[c, :, core, y, zl]
        send("H", c, mine, mine, zpair)

    def I(c):
        arrived(c, "H")
        mine = ACT.at[c, :, core, y]
        send("I0", c, mine, mine, right)
        send("I1", c, mine, mine, left)

    def J(c):
        arrived(c, "I0")
        block = ACT.at[c, :, core, yl, 0]
        send("J0", c, block, block, right)
        arrived(c, "I1")
        block = ACT.at[c, :, core, yr, 1]
        send("J1", c, block, block, left)

    def K(c):
        arrived(c, "J0", "J1")
        mine = ACT.at[c, :, core]
        send("K", c, mine, mine, partner)

    def L(c):
        arrived(c, "K")
        for a in range(2):
            for k in range(2):
                keep(ACT.at[c, a, k], ao.at[a, c, :, :, :, pl.ds(1024 * k, 1024)])

        @pl.loop(0, 2)
        def _(n):
            rows = pl.ds(pl.multiple_of(n * 256, 256), 256)
            part = lax.dot_general(
                ACT[c, 1, 0].reshape(256, 1024), w_in[rows, :1024], NT, preferred_element_type=F32
            )
            part += lax.dot_general(
                ACT[c, 1, 1].reshape(256, 1024), w_in[rows, 1024:], NT, preferred_element_type=F32
            )
            IGP[c, :, :, :, rows] = part.reshape(4, 2, 32, 256)

        for d, kind, piece, half, to in (
            (0, 0, xf, 0, xright), (1, 0, xf, 1, xleft), (0, 1, xr, 1, xright), (1, 1, xl, 0, xleft),
        ):
            send(f"x{d}{kind}", c, IGP.at[c, piece, half], XR.at[c, d, kind], to)

    def M(c):
        for d, piece, half, to in ((0, xr, 0, xright), (1, xl, 1, xleft)):
            arrived(c, f"x{d}0")
            IGP[c, piece, half] = IGP[c, piece, half] + XR[c, d, 0]
            send(f"x{d}2", c, IGP.at[c, piece, half], XR.at[c, d, 2], to)

    def N(c):
        arrived(c, "x01", "x11", "x02", "x12")
        for half in (0, 1):
            IGP[c, x, half] = IGP[c, x, half] + XR[c, 0, 2 - half] + XR[c, 1, 1 + half]
        for j in (1, 2, 3):
            to = (zh + j) % 4
            send(f"N{j}", c, IGP.at[c, x, to // 2, pl.ds(pl.multiple_of((to % 2) * 16, 16), 16)], ZX.at[c, j - 1], zmate[j])

    def O(c):
        arrived(c, "N1", "N2", "N3")
        own_rows = IGP[c, x, zh // 2, pl.ds(pl.multiple_of((zh % 2) * 16, 16), 16)]
        ig_ref[pl.ds(16 * c, 16), :] = (own_rows + ZX[c, 0]) + (ZX[c, 1] + ZX[c, 2])

    theirs, ours = pl.multiple_of((1 - core) * 1024, 1024), pl.multiple_of(core * 1024, 1024)
    A(0)
    send(0, None, w_in.at[:, pl.ds(theirs, 1024)], W1.at[core], partner)
    send(1, None, w_out.at[pl.ds(theirs, 1024), :], W2.at[core], partner)
    own = [
        pltpu.make_async_copy(w_in.at[:, pl.ds(ours, 1024)], W1.at[core], wsem.at[0]),
        pltpu.make_async_copy(w_out.at[pl.ds(ours, 1024), :], W2.at[core], wsem.at[1]),
    ]
    for copy in own:
        copy.start()

    stages = dict(A=A, B=B, C=C, D=D, E=E, F=F, G=G, H=H, I=I, J=J, K=K, L=L, M=M, N=N, O=O)
    order = sorted((at + step * c, name, c) for name, (at, step) in STAGES.items() for c in range(NC))
    for _, name, c in order:
        if (name, c) != ("A", 0):
            stages[name](c)
    for copy in copies.values():
        copy.wait_send()
    for copy in locals_:
        copy.wait()


def local(inputs, out_grad, w_in, w_out):
    vmem = pl.BlockSpec(memory_space=pltpu.VMEM)
    hbm = pl.BlockSpec(memory_space=pl.ANY)
    input_grad, xg, acts = pl.pallas_call(
        kernel,
        out_shape=(
            jax.ShapeDtypeStruct((64, 512), F32),
            jax.ShapeDtypeStruct((2, NC, 16, 16, 512), BF16),
            jax.ShapeDtypeStruct((2, NC, 4, 2, 32, 2048), BF16),
        ),
        in_specs=[vmem] * 4,
        out_specs=(vmem, hbm, hbm),
        scratch_shapes=[
            pltpu.VMEM((NC, 2, 2, 16, 16, 512), BF16),
            pltpu.VMEM((2, 512, 1024), BF16),
            pltpu.VMEM((2, 1024, 512), BF16),
            pltpu.VMEM((NC, 2, 4, 2, 32, 1024), F32),
            pltpu.VMEM((NC, 2, 3, 2, 32, 1024), BF16),
            pltpu.VMEM((NC, 2, 3, 2, 32, 1024), BF16),
            pltpu.VMEM((NC, 2, 32, 1024), BF16),
            pltpu.VMEM((NC, 2, 32, 1024), BF16),
            pltpu.VMEM((NC, 2, 2, 4, 2, 32, 1024), BF16),
            pltpu.VMEM((NC, 4, 2, 32, 512), F32),
            pltpu.VMEM((NC, 2, 3, 32, 512), F32),
            pltpu.VMEM((NC, 3, 16, 512), F32),
            pltpu.SemaphoreType.DMA((NSEM,)),
            pltpu.SemaphoreType.DMA((NSEM,)),
            pltpu.SemaphoreType.DMA((6 * NC,)),
            pltpu.SemaphoreType.DMA((2,)),
        ],
        compiler_params=pltpu.CompilerParams(
            collective_id=0, has_side_effects=True, vmem_limit_bytes=60 * 2**20
        ),
        cost_estimate=pl.CostEstimate(flops=6 * 2**30, bytes_accessed=16 * 2**20, transcendentals=0),
    )(inputs, out_grad, w_in, w_out)
    xg = xg.reshape(2, 1024, 512)
    acts = acts.reshape(2, 1024, 2048)
    tn = (((0,), (0,)), ((), ()))
    w_out_grad = lax.dot_general(acts[0], xg[1], tn, preferred_element_type=F32)
    w_in_grad = lax.dot_general(xg[0], acts[1], tn, preferred_element_type=F32)
    return (input_grad, w_in_grad, w_out_grad)


def solution(mesh):
    return jax.shard_map(
        local,
        mesh=mesh,
        in_specs=(P("hid", "row"), P("hid", "row"), P("row", "hid"), P("hid", "row")),
        out_specs=(P("hid", "row"), P("row", "hid"), P("hid", "row")),
        check_vma=False,
    )
```

time: 504 us -> 169 us (0.34)
  waiting for transfers between devices: 447 us -> 0 us
  Pallas kernels: 0 us -> 153 us
  matrix products: 33.4 us -> 8.93 us
  between operations: 14.2 us -> 0.65 us
    reduce_scatter x3 -> x0, waiting for transfers between devices: 277 us -> none  [the longest x1 101 us: local(): lax.psum_scatter(hidden_part, 'row', scatter_dimension=0, tiled=True)]
    all_gather x4 -> x0, waiting for transfers between devices: 168 us -> none  [the longest x1 57.8 us: local(): lax.all_gather(inputs, 'hid', axis=0, tiled=True)]
    pallas_call x0 -> x1, Pallas kernels: none -> 153 us  [local(): pl.pallas_call(kernel, out_shape=(jax.ShapeDtypeStruct((64, 512), F32), j...]
    dot_general x5 -> x2, matrix products: 33.4 us -> 8.93 us  [the longest x1 4.46 us: local(): w_in_grad = lax.dot_general(xg[0], acts[1], tn, preferred_element_type=F32)]
    slice x0 -> x2, local copies, waits for them, and re-layouts: none -> 5.9 us  [local(): w_out_grad = lax.dot_general(acts[0], xg[1], tn, preferred_element_type=F32)]
  transfers between devices with their start and end apart: 7 -> 0, of which waited for: 7 -> 0; matrix products, arithmetic and copies ran while one was open for 8% -> 0% of each run, Pallas kernels for 0% -> 0%
where the time goes in v1:
time: 169 us
  Pallas kernels  153 us (91%)
  matrix products  8.93 us (5%)
  local copies, waits for them, and re-layouts  6.56 us (4%)
    pallas_call x1, Pallas kernels, local(): pl.pallas_call(kernel, out_shape=(jax.ShapeDtypeStruct((64, 512), F32), j...  153 us
    slice x2, local copies, waits for them, and re-layouts, local(): w_out_grad = lax.dot_general(acts[0], xg[1], tn, preferred_element_type=F32)  5.9 us
    dot_general x1, matrix products, local(): w_in_grad = lax.dot_general(xg[0], acts[1], tn, preferred_element_type=F32)  4.46 us
    dot_general x1, matrix products, local(): w_out_grad = lax.dot_general(acts[0], xg[1], tn, preferred_element_type=F32)  4.46 us

profile of v1, /device:TPU:1, one launch (start us, length us, event | category | flops | bytes accessed | tf_op | source)
XLA Modules:
  0.0 169.3 jit_solution(586525106340003057)
XLA Ops:
  0.6 153.2 %shard_map.67 = (f32[64,512]{1,0:T(8,128)}, bf16[2,4,16,16,512]{4,3,2,1,0:T(8,128)(2,1)}, bf16[2,4,4,2,32,2048]{5,4,3,2,1,0:T(8,128)(2,1)}) custom-call(bf16[64,512]{1,0:T(8,128)(2,1)} %x_ref.1, bf16[64,512]{1,0:T(8,128)(2,1)} %g_ref.1, bf16[512,2048]{1,0:T(8,128)(2,1)} %w_in.1, bf16[2048,512]{1,0:T(8,128)(2,1)} %w_out.1), custom_call_target="tpu_custom_call" | custom-call | flops 6442450944 | bytes 16777216 | tf_op jit(solution)/shard_map/pallas_call | solution.py:258
  153.8 1.7 %fusion.1 = (bf16[1,4,16,16,512]{4,3,2,1,0:T(8,128)(2,1)S(1)}, bf16[1,4,16,16,512]{4,3,2,1,0:T(8,128)(2,1)S(1)}) fusion(bf16[2,4,16,16,512]{4,3,2,1,0:T(8,128)(2,1)} %get-tuple-element.7), kind=kLoop, calls=%fused_computation.1 | loop fusion | bytes 4194304 | tf_op jit(solution)/shard_map/slice | solution.py:293
  155.6 4.2 %fusion = (bf16[1,4,4,2,32,2048]{5,4,3,2,1,0:T(8,128)(2,1)S(1)}, bf16[1,4,4,2,32,2048]{5,4,3,2,1,0:T(8,128)(2,1)S(1)}) fusion(bf16[2,4,4,2,32,2048]{5,4,3,2,1,0:T(8,128)(2,1)} %get-tuple-element.8), kind=kLoop, calls=%fused_computation | loop fusion | bytes 16777216 | tf_op jit(solution)/shard_map/slice | solution.py:293
  159.8 4.5 %fusion.3 = f32[2048,512]{1,0:T(8,128)} fusion(bf16[1024,2048]{1,0:T(8,128)(2,1)S(1)} %bitcast.10, bf16[1024,512]{1,0:T(8,128)(2,1)S(1)} %bitcast.11), kind=kOutput, calls=%fused_computation.3 | convolution fusion | flops 2147483648 | bytes 9437184 | tf_op jit(solution)/shard_map/dot_general | solution.py:293
  164.2 0.0 copy-start
  164.2 4.5 %fusion.2 = f32[512,2048]{1,0:T(8,128)} fusion(bf16[1024,512]{1,0:T(8,128)(2,1)S(1)} %bitcast.9, bf16[1024,2048]{1,0:T(8,128)(2,1)S(1)} %bitcast.8), kind=kOutput, calls=%fused_computation.2 | convolution fusion | flops 2147483648 | bytes 9437184 | tf_op jit(solution)/shard_map/dot_general | solution.py:294
  168.7 0.0 copy-done
  168.7 0.7 copy.8
Async XLA Ops:
  164.2 4.5 %copy-start = (f32[64,512]{1,0:T(8,128)S(1)}, f32[64,512]{1,0:T(8,128)}, u32[]{:S(2)}) copy-start(f32[64,512]{1,0:T(8,128)} %get-tuple-element.16) | copy-start | bytes 393220

commit v2 on v0

v2 whole, which is shorter than its diff:
```python
import jax
import jax.numpy as jnp
from jax import lax
from jax.experimental import pallas as pl
from jax.experimental.pallas import tpu as pltpu
from jax.sharding import PartitionSpec as P

MESH = pl.DeviceIdType.MESH
F32 = jnp.float32
BF16 = jnp.bfloat16
NC = 4
Q = 2
COPIES = 208
NT = (((1,), (1,)), ((), ()))

Z_FIRST = ((0, 1), (1, 1), (2, 1), (3, 1),)
Y_FIRST = ((0, 1), (1, 0), (2, 0),)
ORDER = (
    ("A", 0, 0), ("A", 1, 0), ("A", 2, 0), ("A", 3, 0), ("C0", 0, 0), ("B1", 0, 0),
    ("C0", 1, 0), ("B3", 0, 0), ("C0", 2, 0), ("C0", 3, 0), ("B2", 0, 0), ("B1", 1, 0),
    ("C1", 0, 0), ("C3", 0, 0), ("B3", 1, 0), ("C2", 0, 0), ("B2", 1, 0), ("B1", 2, 0),
    ("B3", 2, 0), ("C3", 1, 0), ("C1", 1, 0), ("B2", 2, 0), ("C2", 1, 0), ("D", 0, 0),
    ("B1", 3, 0), ("B3", 3, 0), ("C3", 2, 0), ("C1", 2, 0), ("B2", 3, 0), ("E", 0, 1),
    ("D", 1, 0), ("C2", 2, 0), ("E", 0, 0), ("C3", 3, 0), ("C1", 3, 0), ("E", 1, 0),
    ("D", 2, 0), ("C2", 3, 0), ("E", 1, 1), ("F1", 0, 0), ("F0", 0, 0), ("E", 2, 0),
    ("D", 3, 0), ("F1", 1, 0), ("e", 0, 1), ("E", 2, 1), ("F0", 1, 0), ("E", 3, 1),
    ("E", 3, 0), ("F1", 2, 0), ("F0", 2, 0), ("G", 0, 0), ("e", 1, 1), ("F0", 0, 1),
    ("F1", 0, 1), ("G", 1, 0), ("F1", 3, 0), ("F0", 3, 0), ("e", 2, 1), ("G", 2, 0),
    ("F1", 1, 1), ("F0", 1, 1), ("H", 0, 1), ("G", 3, 0), ("F1", 2, 1), ("F0", 2, 1),
    ("e", 3, 1), ("H", 1, 1), ("H", 0, 0), ("J0", 0, 1), ("J1", 0, 1), ("H", 1, 0),
    ("H", 2, 1), ("F1", 3, 1), ("F0", 3, 1), ("H", 2, 0), ("k", 0, 1), ("H", 3, 0),
    ("J0", 1, 0), ("J1", 1, 0), ("I", 1, 1), ("H", 3, 1), ("I", 0, 0), ("J0", 2, 0),
    ("J1", 2, 0), ("k", 1, 0), ("I", 2, 1), ("J0", 1, 1), ("J1", 1, 1), ("J0", 0, 0),
    ("J1", 0, 0), ("K", 0, 1), ("k", 2, 0), ("I", 3, 0), ("I", 3, 1), ("J0", 2, 1),
    ("J1", 2, 1), ("K", 1, 1), ("K", 0, 0), ("K", 1, 0), ("L", 0, 0), ("J0", 3, 0),
    ("J1", 3, 0), ("L", 0, 1), ("L", 1, 0), ("L", 1, 1), ("J0", 3, 1), ("J1", 3, 1),
    ("M0", 0, 1), ("M1", 0, 1), ("K", 2, 1), ("K", 2, 0), ("M0", 1, 1), ("M1", 1, 1),
    ("K", 3, 0), ("N", 0, 1), ("K", 3, 1), ("L", 2, 0), ("L", 2, 1), ("L", 3, 0),
    ("N", 1, 1), ("L", 3, 1), ("O", 0, 1), ("M0", 2, 1), ("M1", 2, 1), ("O", 1, 1),
    ("M0", 3, 1), ("M1", 3, 1), ("N", 2, 1), ("N", 3, 1), ("O", 2, 1), ("O", 3, 1),
)


def gelu_parts(pre):
    phi = 0.5 * (1.0 + lax.erf(pre * 0.7071067811865476))
    dens = jnp.exp(-0.5 * pre * pre) * 0.3989422804014327
    return (pre * phi, phi + pre * dens)


UP, DOWN = 2.0**50, 2.0**-50
UP_IG, DOWN_IG = 2.0**40, 2.0**-40


def encode(v, up=UP):
    return ((v * up) * (jnp.abs(v) * up)).astype(BF16)


def decode(q, down=DOWN):
    q = q.astype(F32)
    root = jnp.sqrt(jnp.abs(q)) * down
    return jnp.where(q < 0, -root, root)


def kernel(x_ref, g_ref, w_in, w_out, ig_ref, xo, ao,
           XG, WV, W1, W2, PT, TX, RX, ZT, ZR, ACT, IGP, XT, XR, NX, ZX, ssem, rsem, lsem, wsem):
    r, h = lax.axis_index("row"), lax.axis_index("hid")
    core, zl, y = r % 2, (r // 2) % 2, r // 4
    x, zh = h // 4, h % 4

    def dev(y=y, zl=zl, core=core, x=x, zh=zh):
        return {"row": (y * 2 + zl) * 2 + core, "hid": x * 4 + zh}

    yr, yl, yf = (y + 1) % 4, (y + 3) % 4, (y + 2) % 4
    xr, xl, xf = (x + 1) % 4, (x + 3) % 4, (x + 2) % 4
    right, left = dev(y=yr), dev(y=yl)
    xright, xleft = dev(x=xr), dev(x=xl)
    partner, zpair = dev(core=1 - core), dev(zl=1 - zl)
    zmate = {j: dev(zh=(zh + j) % 4) for j in (1, 2, 3)}
    behind = {j: (zh + 4 - j) % 4 for j in (0, 1, 2, 3)}

    barrier = pltpu.get_barrier_semaphore()
    others = [right, left, xright, xleft, partner, zpair, zmate[1], zmate[2], zmate[3]]
    for other in others:
        pl.semaphore_signal(barrier, inc=1, device_id=other, device_id_type=MESH)
    pl.semaphore_wait(barrier, len(others))

    copies = {}
    locals_ = []

    def send(key, src, dst, to):
        i = len(copies)
        copy = pltpu.make_async_remote_copy(
            src_ref=src, dst_ref=dst, send_sem=ssem.at[i], recv_sem=rsem.at[i], device_id=to, device_id_type=MESH
        )
        copy.start()
        copies[key] = copy

    def arrived(*keys):
        for key in keys:
            copies[key].wait_recv()

    def keep(src, dst):
        copy = pltpu.make_async_copy(src, dst, lsem.at[len(locals_)])
        copy.start()
        locals_.append(copy)

    def A(c, u):
        rows = pl.ds(16 * c, 16)
        XG[c, 0, core, h] = x_ref[rows, :]
        XG[c, 1, core, h] = g_ref[rows, :]
        mine = XG.at[c, :, core, h]
        for j in (1, 3, 2):
            send((f"A{j}", c), mine, mine, zmate[j])
        send(("B0r", c), mine, mine, xright)
        send(("B0l", c), mine, mine, xleft)

    def B(j, c):
        arrived((f"A{j}", c))
        block = XG.at[c, :, core, 4 * x + behind[j]]
        send((f"B{j}r", c), block, block, xright)
        send((f"B{j}l", c), block, block, xleft)

    def C(j, c):
        if j < 2:
            arrived((f"B{j}r", c))
            block = XG.at[c, :, core, 4 * xl + behind[j]]
            send((f"C{j}", c), block, block, xright)
        else:
            arrived((f"B{j}l", c))
            block = XG.at[c, :, core, 4 * xr + behind[j]]
            send((f"C{j}", c), block, block, xleft)

    def D(c, u):
        arrived(("C0", c), ("C1", c), ("C2", c), ("C3", c), ("B2r", c), ("B3r", c), ("B0l", c), ("B1l", c))
        mine = XG.at[c, :, core]
        send(("D", c), mine, mine, partner)
        for a in range(2):
            keep(XG.at[c, a, core], xo.at[a, c])

    ready = []

    def E(c, u):
        if not ready:
            arrived("w_in", "w_out")
            for copy in own:
                copy.wait()
        if ("D", c) not in ready:
            arrived(("D", c))
        ready.append(("D", c))

        @pl.loop(0, 2)
        def _(n):
            cols = pl.ds(pl.multiple_of(n * 256, 256), 256)
            wide = pl.ds(pl.multiple_of(n * 256 + 512 * u, 256), 256)
            pre = jnp.dot(XG[c, 0, 0].reshape(256, 512), W1[0, :, wide], preferred_element_type=F32)
            pre += jnp.dot(XG[c, 0, 1].reshape(256, 512), W1[1, :, wide], preferred_element_type=F32)
            PT[c, u, 0, :, :, :, cols] = pre.reshape(4, 2, 32, 256)
            hid = lax.dot_general(XG[c, 1, 0].reshape(256, 512), W2[0, wide, :], NT, preferred_element_type=F32)
            hid += lax.dot_general(XG[c, 1, 1].reshape(256, 512), W2[1, wide, :], NT, preferred_element_type=F32)
            PT[c, u, 1, :, :, :, cols] = hid.reshape(4, 2, 32, 256)

        if (c, u) in Z_FIRST:
            for a in range(2):
                ZT[c, u, a] = encode(PT[c, u, a, :, 1 - zl])
            send(("z", c, u), ZT.at[c, u], ZR.at[c, u], zpair)
        else:
            tree(c, u)

    def e(c, u):
        arrived(("z", c, u))
        for a in range(2):
            PT[c, u, a, :, zl] = PT[c, u, a, :, zl] + decode(ZR[c, u, a])
        tree(c, u)

    def part(c, u, a, piece, half):
        if (c, u) in Z_FIRST:
            return PT.at[c, u, a, piece, zl, pl.ds(16 * half, 16)]
        return PT.at[c, u, a, piece, half]

    def rows_of(c, u):
        return pl.ds(0, 16 if (c, u) in Z_FIRST else 32)

    def tree(c, u):
        rows = rows_of(c, u)
        for d, kind, piece, half, to in (
            (0, 0, yf, 0, right), (1, 0, yf, 1, left), (0, 1, yr, 1, right), (1, 1, yl, 0, left),
        ):
            for a in range(2):
                TX[c, u, d, kind, a, rows] = encode(part(c, u, a, piece, half)[...])
            send((f"y{d}{kind}", c, u), TX.at[c, u, d, kind, :, rows], RX.at[c, u, d, kind, :, rows], to)

    def F(d, c, u):
        rows = rows_of(c, u)
        piece, half, to = ((yr, 0, right), (yl, 1, left))[d]
        arrived((f"y{d}0", c, u))
        for a in range(2):
            TX[c, u, d, 2, a, rows] = encode(part(c, u, a, piece, half)[...] + decode(RX[c, u, d, 0, a, rows]))
        send((f"y{d}2", c, u), TX.at[c, u, d, 2, :, rows], RX.at[c, u, d, 2, :, rows], to)

    def own_sum(c, u, a, half):
        rows = rows_of(c, u)
        return (
            part(c, u, a, y, half)[...]
            + decode(RX[c, u, 0, 2 - half, a, rows])
            + decode(RX[c, u, 1, 1 + half, a, rows])
        )

    def G(c, u):
        arrived(*((f"y{d}{kind}", c, u) for d in range(2) for kind in (1, 2)))
        for a in range(2):
            ZT[c, u, a, 0] = encode(own_sum(c, u, a, 1 - zl))
        send(("z", c, u), ZT.at[c, u, :, 0], ZR.at[c, u, :, 0], zpair)
        for a in range(2):
            PT[c, u, a, y, zl] = own_sum(c, u, a, zl)

    def H(c, u):
        if (c, u) in Z_FIRST:
            arrived(*((f"y{d}{kind}", c, u) for d in range(2) for kind in (1, 2)))
            for half in range(2):
                rows = pl.ds(16 * half, 16)
                value, slope = gelu_parts(own_sum(c, u, 0, half))
                ACT[c, 0, core, u, y, zl, rows] = value.astype(BF16)
                ACT[c, 1, core, u, y, zl, rows] = (own_sum(c, u, 1, half) * slope).astype(BF16)
        else:
            arrived(("z", c, u))
            value, slope = gelu_parts(PT[c, u, 0, y, zl] + decode(ZR[c, u, 0, 0]))
            hidden = PT[c, u, 1, y, zl] + decode(ZR[c, u, 1, 0])
            ACT[c, 0, core, u, y, zl] = value.astype(BF16)
            ACT[c, 1, core, u, y, zl] = (hidden * slope).astype(BF16)
        mine = ACT.at[c, :, core, u, y, zl]
        if (c, u) in Y_FIRST:
            send(("I0", c, u), mine, mine, right)
            send(("I1", c, u), mine, mine, left)
        else:
            send(("H", c, u), mine, mine, zpair)

    def I(c, u):
        arrived(("H", c, u))
        mine = ACT.at[c, :, core, u, y]
        send(("I0", c, u), mine, mine, right)
        send(("I1", c, u), mine, mine, left)

    def J(d, c, u):
        arrived((f"I{d}", c, u))
        piece, to = ((yl, right), (yr, left))[d]
        if (c, u) in Y_FIRST:
            block = ACT.at[c, :, core, u, piece, zl, pl.ds(16 * d, 16)]
        else:
            block = ACT.at[c, :, core, u, piece, d]
        send((f"J{d}", c, u), block, block, to)

    def k(c, u):
        arrived(("J0", c, u), ("J1", c, u))
        mine = ACT.at[c, :, core, u, :, zl]
        send(("k", c, u), mine, mine, zpair)

    def K(c, u):
        arrived(*([("k", c, u)] if (c, u) in Y_FIRST else [("J0", c, u), ("J1", c, u)]))
        mine = ACT.at[c, :, core, u]
        send(("K", c, u), mine, mine, partner)

    def L(c, u):
        arrived(("K", c, u))
        for a in range(2):
            for half in range(2):
                keep(ACT.at[c, a, half, u], ao.at[a, c, :, :, :, pl.ds(1024 * half + 512 * u, 512)])

        @pl.loop(0, 2)
        def _(n):
            rows = pl.ds(pl.multiple_of(n * 256, 256), 256)
            total = jnp.zeros((256, 256), F32)
            for half in range(2):
                total += lax.dot_general(
                    ACT[c, 1, half, u].reshape(256, 512), WV[rows, pl.ds(1024 * half + 512 * u, 512)], NT,
                    preferred_element_type=F32,
                )
            total = total.reshape(4, 2, 32, 256)
            IGP[c, :, :, :, rows] = total if u == 0 else IGP[c, :, :, :, rows] + total

        if u == 0:
            return
        for d, kind, piece, half, to in (
            (0, 0, xf, 0, xright), (1, 0, xf, 1, xleft), (0, 1, xr, 1, xright), (1, 1, xl, 0, xleft),
        ):
            XT[c, d, kind] = encode(IGP[c, piece, half], UP_IG)
            send((f"x{d}{kind}", c), XT.at[c, d, kind], XR.at[c, d, kind], to)

    def M(d, c):
        piece, half, to = ((xr, 0, xright), (xl, 1, xleft))[d]
        arrived((f"x{d}0", c))
        XT[c, d, 2] = encode(IGP[c, piece, half] + decode(XR[c, d, 0], DOWN_IG), UP_IG)
        send((f"x{d}2", c), XT.at[c, d, 2], XR.at[c, d, 2], to)

    def N(c, u):
        arrived(*((f"x{d}{kind}", c) for d in range(2) for kind in (1, 2)))
        for half in (0, 1):
            IGP[c, x, half] = (
                IGP[c, x, half] + decode(XR[c, 0, 2 - half], DOWN_IG) + decode(XR[c, 1, 1 + half], DOWN_IG)
            )
        for j in (1, 2, 3):
            NX[c, j - 1] = encode(rows_for(c, (zh + j) % 4), UP_IG)
            send((f"N{j}", c), NX.at[c, j - 1], ZX.at[c, j - 1], zmate[j])

    def rows_for(c, to):
        return IGP[c, x, to // 2, pl.ds(pl.multiple_of((to % 2) * 16, 16), 16)]

    def O(c, u):
        arrived(("N1", c), ("N2", c), ("N3", c))
        others = decode(ZX[c, 0], DOWN_IG) + decode(ZX[c, 1], DOWN_IG) + decode(ZX[c, 2], DOWN_IG)
        ig_ref[pl.ds(16 * c, 16), :] = rows_for(c, zh) + others

    stages = dict(A=A, D=D, E=E, e=e, G=G, H=H, I=I, k=k, K=K, L=L, N=N, O=O)
    for j in (1, 2, 3):
        stages[f"B{j}"] = lambda c, u, j=j: B(j, c)
    for j in range(4):
        stages[f"C{j}"] = lambda c, u, j=j: C(j, c)
    for d in range(2):
        stages[f"F{d}"] = lambda c, u, d=d: F(d, c, u)
        stages[f"J{d}"] = lambda c, u, d=d: J(d, c, u)
        stages[f"M{d}"] = lambda c, u, d=d: M(d, c)

    theirs, ours = pl.multiple_of((1 - core) * 1024, 1024), pl.multiple_of(core * 1024, 1024)
    own = [
        pltpu.make_async_copy(w_in.at[:, pl.ds(ours, 1024)], W1.at[core], wsem.at[0]),
        pltpu.make_async_copy(w_out.at[pl.ds(ours, 1024), :], W2.at[core], wsem.at[1]),
        pltpu.make_async_copy(w_in, WV, wsem.at[2]),
    ]
    for i, (stage, c, u) in enumerate(ORDER):
        stages[stage](c, u)
        if i == 0:
            send("w_in", w_in.at[:, pl.ds(theirs, 1024)], W1.at[core], partner)
            send("w_out", w_out.at[pl.ds(theirs, 1024), :], W2.at[core], partner)
            for copy in own:
                copy.start()
    for copy in copies.values():
        copy.wait_send()
    for copy in locals_:
        copy.wait()


def local(inputs, out_grad, w_in, w_out):
    vmem = pl.BlockSpec(memory_space=pltpu.VMEM)
    hbm = pl.BlockSpec(memory_space=pl.ANY)
    input_grad, xg, acts = pl.pallas_call(
        kernel,
        out_shape=(
            jax.ShapeDtypeStruct((64, 512), F32),
            jax.ShapeDtypeStruct((2, NC, 16, 16, 512), BF16),
            jax.ShapeDtypeStruct((2, NC, 4, 2, 32, 2048), BF16),
        ),
        in_specs=[vmem, vmem, hbm, hbm],
        out_specs=(vmem, hbm, hbm),
        scratch_shapes=[
            pltpu.VMEM((NC, 2, 2, 16, 16, 512), BF16),
            pltpu.VMEM((512, 2048), BF16),
            pltpu.VMEM((2, 512, 1024), BF16),
            pltpu.VMEM((2, 1024, 512), BF16),
            pltpu.VMEM((NC, Q, 2, 4, 2, 32, 512), F32),
            pltpu.VMEM((NC, Q, 2, 3, 2, 32, 512), BF16),
            pltpu.VMEM((NC, Q, 2, 3, 2, 32, 512), BF16),
            pltpu.VMEM((NC, Q, 2, 4, 32, 512), BF16),
            pltpu.VMEM((NC, Q, 2, 4, 32, 512), BF16),
            pltpu.VMEM((NC, 2, 2, Q, 4, 2, 32, 512), BF16),
            pltpu.VMEM((NC, 4, 2, 32, 512), F32),
            pltpu.VMEM((NC, 2, 3, 32, 512), BF16),
            pltpu.VMEM((NC, 2, 3, 32, 512), BF16),
            pltpu.VMEM((NC, 3, 16, 512), BF16),
            pltpu.VMEM((NC, 3, 16, 512), BF16),
            pltpu.SemaphoreType.DMA((COPIES,)),
            pltpu.SemaphoreType.DMA((COPIES,)),
            pltpu.SemaphoreType.DMA((10 * NC,)),
            pltpu.SemaphoreType.DMA((3,)),
        ],
        compiler_params=pltpu.CompilerParams(
            collective_id=0, has_side_effects=True, vmem_limit_bytes=60 * 2**20
        ),
        cost_estimate=pl.CostEstimate(flops=6 * 2**30, bytes_accessed=16 * 2**20, transcendentals=0),
    )(inputs, out_grad, w_in, w_out)
    xg = xg.reshape(2, 1024, 512)
    acts = acts.reshape(2, 1024, 2048)
    tn = (((0,), (0,)), ((), ()))
    w_out_grad = lax.dot_general(acts[0], xg[1], tn, preferred_element_type=F32)
    w_in_grad = lax.dot_general(xg[0], acts[1], tn, preferred_element_type=F32)
    return (input_grad, w_in_grad, w_out_grad)


def solution(mesh):
    return jax.shard_map(
        local,
        mesh=mesh,
        in_specs=(P("hid", "row"), P("hid", "row"), P("row", "hid"), P("hid", "row")),
        out_specs=(P("hid", "row"), P("row", "hid"), P("hid", "row")),
        check_vma=False,
    )
```

time: 504 us -> 123 us (0.24)
  waiting for transfers between devices: 447 us -> 0 us
  Pallas kernels: 0 us -> 106 us
  matrix products: 33.4 us -> 8.93 us
  between operations: 14.2 us -> 0.65 us
    reduce_scatter x3 -> x0, waiting for transfers between devices: 277 us -> none  [the longest x1 101 us: local(): lax.psum_scatter(hidden_part, 'row', scatter_dimension=0, tiled=True)]
    all_gather x4 -> x0, waiting for transfers between devices: 168 us -> none  [the longest x1 57.8 us: local(): lax.all_gather(inputs, 'hid', axis=0, tiled=True)]
    pallas_call x0 -> x1, Pallas kernels: none -> 106 us  [local(): pl.pallas_call(kernel, out_shape=(jax.ShapeDtypeStruct((64, 512), F32), j...]
    dot_general x5 -> x2, matrix products: 33.4 us -> 8.93 us  [the longest x1 4.47 us: local(): w_in_grad = lax.dot_general(xg[0], acts[1], tn, preferred_element_type=F32)]
    slice x0 -> x2, local copies, waits for them, and re-layouts: none -> 5.72 us  [local(): w_out_grad = lax.dot_general(acts[0], xg[1], tn, preferred_element_type=F32)]
  transfers between devices with their start and end apart: 7 -> 0, of which waited for: 7 -> 0; matrix products, arithmetic and copies ran while one was open for 8% -> 0% of each run, Pallas kernels for 0% -> 0%
where the time goes in v2:
time: 123 us; the launch traced here: 121 us
  Pallas kernels  106 us (86%)
  matrix products  8.93 us (7%)
  local copies, waits for them, and re-layouts  6.38 us (5%)
    pallas_call x1, Pallas kernels, local(): pl.pallas_call(kernel, out_shape=(jax.ShapeDtypeStruct((64, 512), F32), j...  106 us
    slice x2, local copies, waits for them, and re-layouts, local(): w_out_grad = lax.dot_general(acts[0], xg[1], tn, preferred_element_type=F32)  5.72 us
    dot_general x1, matrix products, local(): w_in_grad = lax.dot_general(xg[0], acts[1], tn, preferred_element_type=F32)  4.47 us
    dot_general x1, matrix products, local(): w_out_grad = lax.dot_general(acts[0], xg[1], tn, preferred_element_type=F32)  4.46 us

profile of v2, /device:TPU:1, one launch (start us, length us, event | category | flops | bytes accessed | tf_op | source)
XLA Modules:
  0.0 121.5 jit_solution(9058899598038852671)
XLA Ops:
  0.6 105.5 %shard_map.67 = (f32[64,512]{1,0:T(8,128)}, bf16[2,4,16,16,512]{4,3,2,1,0:T(8,128)(2,1)}, bf16[2,4,4,2,32,2048]{5,4,3,2,1,0:T(8,128)(2,1)}) custom-call(bf16[64,512]{1,0:T(8,128)(2,1)} %x_ref.1, bf16[64,512]{1,0:T(8,128)(2,1)} %g_ref.1, bf16[512,2048]{1,0:T(8,128)(2,1)} %w_in.1, bf16[2048,512]{1,0:T(8,128)(2,1)} %w_out.1), custom_call_target="tpu_custom_call" | custom-call | flops 6442450944 | bytes 16777216 | tf_op jit(solution)/shard_map/pallas_call | solution.py:344
  106.2 1.7 %fusion.1 = (bf16[1,4,16,16,512]{4,3,2,1,0:T(8,128)(2,1)S(1)}, bf16[1,4,16,16,512]{4,3,2,1,0:T(8,128)(2,1)S(1)}) fusion(bf16[2,4,16,16,512]{4,3,2,1,0:T(8,128)(2,1)} %get-tuple-element.7), kind=kLoop, calls=%fused_computation.1 | loop fusion | bytes 4194304 | tf_op jit(solution)/shard_map/slice | solution.py:382
  107.9 4.0 %fusion = (bf16[1,4,4,2,32,2048]{5,4,3,2,1,0:T(8,128)(2,1)S(1)}, bf16[1,4,4,2,32,2048]{5,4,3,2,1,0:T(8,128)(2,1)S(1)}) fusion(bf16[2,4,4,2,32,2048]{5,4,3,2,1,0:T(8,128)(2,1)} %get-tuple-element.8), kind=kLoop, calls=%fused_computation | loop fusion | bytes 16777216 | tf_op jit(solution)/shard_map/slice | solution.py:382
  111.9 4.5 %fusion.3 = f32[2048,512]{1,0:T(8,128)} fusion(bf16[1024,2048]{1,0:T(8,128)(2,1)S(1)} %bitcast.10, bf16[1024,512]{1,0:T(8,128)(2,1)S(1)} %bitcast.11), kind=kOutput, calls=%fused_computation.3 | convolution fusion | flops 2147483648 | bytes 9437184 | tf_op jit(solution)/shard_map/dot_general | solution.py:382
  116.4 0.0 copy-start
  116.4 4.5 %fusion.2 = f32[512,2048]{1,0:T(8,128)} fusion(bf16[1024,512]{1,0:T(8,128)(2,1)S(1)} %bitcast.9, bf16[1024,2048]{1,0:T(8,128)(2,1)S(1)} %bitcast.8), kind=kOutput, calls=%fused_computation.2 | convolution fusion | flops 2147483648 | bytes 9437184 | tf_op jit(solution)/shard_map/dot_general | solution.py:383
  120.8 0.0 copy-done
  120.8 0.7 copy.8
Async XLA Ops:
  116.4 4.5 %copy-start = (f32[64,512]{1,0:T(8,128)S(1)}, f32[64,512]{1,0:T(8,128)}, u32[]{:S(2)}) copy-start(f32[64,512]{1,0:T(8,128)} %get-tuple-element.16) | copy-start | bytes 393220

commit v3 on v2

--- a/solution.py
+++ b/solution.py
@@ -12,32 +12,29 @@
 Q = 2
 COPIES = 208
 NT = (((1,), (1,)), ((), ()))
-
-Z_FIRST = ((0, 1), (1, 1), (2, 1), (3, 1),)
-Y_FIRST = ((0, 1), (1, 0), (2, 0),)
+TN = (((0,), (0,)), ((), ()))
+
+Z_FIRST = ((1, 1), (2, 0), (3, 0),)
+Y_FIRST = ((0, 0), (1, 1), (2, 1),)
 ORDER = (
-    ("A", 0, 0), ("A", 1, 0), ("A", 2, 0), ("A", 3, 0), ("C0", 0, 0), ("B1", 0, 0),
-    ("C0", 1, 0), ("B3", 0, 0), ("C0", 2, 0), ("C0", 3, 0), ("B2", 0, 0), ("B1", 1, 0),
-    ("C1", 0, 0), ("C3", 0, 0), ("B3", 1, 0), ("C2", 0, 0), ("B2", 1, 0), ("B1", 2, 0),
-    ("B3", 2, 0), ("C3", 1, 0), ("C1", 1, 0), ("B2", 2, 0), ("C2", 1, 0), ("D", 0, 0),
-    ("B1", 3, 0), ("B3", 3, 0), ("C3", 2, 0), ("C1", 2, 0), ("B2", 3, 0), ("E", 0, 1),
-    ("D", 1, 0), ("C2", 2, 0), ("E", 0, 0), ("C3", 3, 0), ("C1", 3, 0), ("E", 1, 0),
-    ("D", 2, 0), ("C2", 3, 0), ("E", 1, 1), ("F1", 0, 0), ("F0", 0, 0), ("E", 2, 0),
-    ("D", 3, 0), ("F1", 1, 0), ("e", 0, 1), ("E", 2, 1), ("F0", 1, 0), ("E", 3, 1),
-    ("E", 3, 0), ("F1", 2, 0), ("F0", 2, 0), ("G", 0, 0), ("e", 1, 1), ("F0", 0, 1),
-    ("F1", 0, 1), ("G", 1, 0), ("F1", 3, 0), ("F0", 3, 0), ("e", 2, 1), ("G", 2, 0),
-    ("F1", 1, 1), ("F0", 1, 1), ("H", 0, 1), ("G", 3, 0), ("F1", 2, 1), ("F0", 2, 1),
-    ("e", 3, 1), ("H", 1, 1), ("H", 0, 0), ("J0", 0, 1), ("J1", 0, 1), ("H", 1, 0),
-    ("H", 2, 1), ("F1", 3, 1), ("F0", 3, 1), ("H", 2, 0), ("k", 0, 1), ("H", 3, 0),
-    ("J0", 1, 0), ("J1", 1, 0), ("I", 1, 1), ("H", 3, 1), ("I", 0, 0), ("J0", 2, 0),
-    ("J1", 2, 0), ("k", 1, 0), ("I", 2, 1), ("J0", 1, 1), ("J1", 1, 1), ("J0", 0, 0),
-    ("J1", 0, 0), ("K", 0, 1), ("k", 2, 0), ("I", 3, 0), ("I", 3, 1), ("J0", 2, 1),
-    ("J1", 2, 1), ("K", 1, 1), ("K", 0, 0), ("K", 1, 0), ("L", 0, 0), ("J0", 3, 0),
-    ("J1", 3, 0), ("L", 0, 1), ("L", 1, 0), ("L", 1, 1), ("J0", 3, 1), ("J1", 3, 1),
-    ("M0", 0, 1), ("M1", 0, 1), ("K", 2, 1), ("K", 2, 0), ("M0", 1, 1), ("M1", 1, 1),
-    ("K", 3, 0), ("N", 0, 1), ("K", 3, 1), ("L", 2, 0), ("L", 2, 1), ("L", 3, 0),
-    ("N", 1, 1), ("L", 3, 1), ("O", 0, 1), ("M0", 2, 1), ("M1", 2, 1), ("O", 1, 1),
-    ("M0", 3, 1), ("M1", 3, 1), ("N", 2, 1), ("N", 3, 1), ("O", 2, 1), ("O", 3, 1),
+    ("A", 0, 0), ("A", 1, 0), ("B1", 0, 0), ("B3", 0, 0), ("B2", 0, 0), ("B1", 1, 0),
+    ("B3", 1, 0), ("B2", 1, 0), ("A", 2, 0), ("D", 0, 0), ("B1", 2, 0), ("E", 0, 0),
+    ("B3", 2, 0), ("D", 1, 0), ("B2", 2, 0), ("A", 3, 0), ("E", 0, 1), ("F0", 0, 0),
+    ("E", 1, 1), ("B1", 3, 0), ("F1", 0, 0), ("B3", 3, 0), ("D", 2, 0), ("B2", 3, 0),
+    ("F1", 0, 1), ("F0", 0, 1), ("E", 1, 0), ("E", 2, 1), ("G", 0, 0), ("E", 2, 0),
+    ("D", 3, 0), ("e", 1, 1), ("G", 0, 1), ("F1", 1, 0), ("F0", 1, 0), ("H", 0, 0),
+    ("E", 3, 1), ("E", 3, 0), ("F1", 2, 1), ("F0", 2, 1), ("F0", 1, 1), ("F1", 1, 1),
+    ("G", 1, 0), ("e", 2, 0), ("J0", 0, 0), ("J1", 0, 0), ("H", 0, 1), ("F0", 3, 1),
+    ("F1", 3, 1), ("G", 2, 1), ("H", 1, 1), ("F0", 2, 0), ("F1", 2, 0), ("e", 3, 0),
+    ("k", 0, 0), ("H", 1, 0), ("G", 3, 1), ("I", 0, 1), ("J0", 1, 1), ("J1", 1, 1),
+    ("H", 2, 1), ("H", 2, 0), ("F0", 3, 0), ("F1", 3, 0), ("J0", 0, 1), ("J1", 0, 1),
+    ("k", 1, 1), ("K", 0, 0), ("J0", 2, 1), ("J1", 2, 1), ("I", 1, 0), ("H", 3, 0),
+    ("L", 0, 0), ("H", 3, 1), ("K", 0, 1), ("k", 2, 1), ("I", 2, 0), ("L", 0, 1),
+    ("J0", 1, 0), ("J1", 1, 0), ("J0", 2, 0), ("J1", 2, 0), ("K", 1, 1), ("K", 1, 0),
+    ("I", 3, 0), ("N", 0, 1), ("I", 3, 1), ("K", 2, 0), ("L", 1, 0), ("L", 1, 1),
+    ("L", 2, 0), ("J0", 3, 0), ("J1", 3, 0), ("K", 2, 1), ("J0", 3, 1), ("J1", 3, 1),
+    ("O", 0, 1), ("N", 1, 1), ("K", 3, 0), ("L", 2, 1), ("K", 3, 1), ("L", 3, 0),
+    ("O", 1, 1), ("L", 3, 1), ("N", 2, 1), ("O", 2, 1), ("N", 3, 1), ("O", 3, 1),
 )
 
 
@@ -61,7 +58,7 @@
     return jnp.where(q < 0, -root, root)
 
 
-def kernel(x_ref, g_ref, w_in, w_out, ig_ref, xo, ao,
+def kernel(x_ref, g_ref, w_in, w_out, ig_ref, xo, go, ao, po,
            XG, WV, W1, W2, PT, TX, RX, ZT, ZR, ACT, IGP, XT, XR, NX, ZX, ssem, rsem, lsem, wsem):
     r, h = lax.axis_index("row"), lax.axis_index("hid")
     core, zl, y = r % 2, (r // 2) % 2, r // 4
@@ -71,15 +68,14 @@
         return {"row": (y * 2 + zl) * 2 + core, "hid": x * 4 + zh}
 
     yr, yl, yf = (y + 1) % 4, (y + 3) % 4, (y + 2) % 4
-    xr, xl, xf = (x + 1) % 4, (x + 3) % 4, (x + 2) % 4
     right, left = dev(y=yr), dev(y=yl)
-    xright, xleft = dev(x=xr), dev(x=xl)
     partner, zpair = dev(core=1 - core), dev(zl=1 - zl)
+    xmate = {j: dev(x=(x + j) % 4) for j in (1, 2, 3)}
     zmate = {j: dev(zh=(zh + j) % 4) for j in (1, 2, 3)}
     behind = {j: (zh + 4 - j) % 4 for j in (0, 1, 2, 3)}
 
     barrier = pltpu.get_barrier_semaphore()
-    others = [right, left, xright, xleft, partner, zpair, zmate[1], zmate[2], zmate[3]]
+    others = [right, left, partner, zpair, *xmate.values(), *zmate.values()]
     for other in others:
         pl.semaphore_signal(barrier, inc=1, device_id=other, device_id_type=MESH)
     pl.semaphore_wait(barrier, len(others))
@@ -111,31 +107,23 @@
         mine = XG.at[c, :, core, h]
         for j in (1, 3, 2):
             send((f"A{j}", c), mine, mine, zmate[j])
-        send(("B0r", c), mine, mine, xright)
-        send(("B0l", c), mine, mine, xleft)
+        across(0, c)
+
+    def across(j, c):
+        block = XG.at[c, :, core, 4 * x + behind[j]]
+        for i in (1, 3, 2):
+            send((f"B{j}{i}", c), block, block, xmate[i])
 
     def B(j, c):
         arrived((f"A{j}", c))
-        block = XG.at[c, :, core, 4 * x + behind[j]]
-        send((f"B{j}r", c), block, block, xright)
-        send((f"B{j}l", c), block, block, xleft)
-
-    def C(j, c):
-        if j < 2:
-            arrived((f"B{j}r", c))
-            block = XG.at[c, :, core, 4 * xl + behind[j]]
-            send((f"C{j}", c), block, block, xright)
-        else:
-            arrived((f"B{j}l", c))
-            block = XG.at[c, :, core, 4 * xr + behind[j]]
-            send((f"C{j}", c), block, block, xleft)
+        across(j, c)
 
     def D(c, u):
-        arrived(("C0", c), ("C1", c), ("C2", c), ("C3", c), ("B2r", c), ("B3r", c), ("B0l", c), ("B1l", c))
+        arrived(*((f"B{j}{i}", c) for j in range(4) for i in (1, 2, 3)))
         mine = XG.at[c, :, core]
         send(("D", c), mine, mine, partner)
-        for a in range(2):
-            keep(XG.at[c, a, core], xo.at[a, c])
+        keep(XG.at[c, 0, core], xo.at[c])
+        keep(XG.at[c, 1, core], go.at[c])
 
     ready = []
 
@@ -263,7 +251,7 @@
         arrived(("K", c, u))
         for a in range(2):
             for half in range(2):
-                keep(ACT.at[c, a, half, u], ao.at[a, c, :, :, :, pl.ds(1024 * half + 512 * u, 512)])
+                keep(ACT.at[c, a, half, u], (ao, po)[a].at[c, :, :, :, pl.ds(1024 * half + 512 * u, 512)])
 
         @pl.loop(0, 2)
         def _(n):
@@ -279,24 +267,14 @@
 
         if u == 0:
             return
-        for d, kind, piece, half, to in (
-            (0, 0, xf, 0, xright), (1, 0, xf, 1, xleft), (0, 1, xr, 1, xright), (1, 1, xl, 0, xleft),
-        ):
-            XT[c, d, kind] = encode(IGP[c, piece, half], UP_IG)
-            send((f"x{d}{kind}", c), XT.at[c, d, kind], XR.at[c, d, kind], to)
-
-    def M(d, c):
-        piece, half, to = ((xr, 0, xright), (xl, 1, xleft))[d]
-        arrived((f"x{d}0", c))
-        XT[c, d, 2] = encode(IGP[c, piece, half] + decode(XR[c, d, 0], DOWN_IG), UP_IG)
-        send((f"x{d}2", c), XT.at[c, d, 2], XR.at[c, d, 2], to)
+        for j in (1, 3, 2):
+            XT[c, j - 1] = encode(IGP[c, (x + j) % 4], UP_IG)
+            send((f"x{j}", c), XT.at[c, j - 1], XR.at[c, j - 1], xmate[j])
 
     def N(c, u):
-        arrived(*((f"x{d}{kind}", c) for d in range(2) for kind in (1, 2)))
-        for half in (0, 1):
-            IGP[c, x, half] = (
-                IGP[c, x, half] + decode(XR[c, 0, 2 - half], DOWN_IG) + decode(XR[c, 1, 1 + half], DOWN_IG)
-            )
+        arrived(("x1", c), ("x2", c), ("x3", c))
+        others = decode(XR[c, 0], DOWN_IG) + decode(XR[c, 1], DOWN_IG) + decode(XR[c, 2], DOWN_IG)
+        IGP[c, x] = IGP[c, x] + others
         for j in (1, 2, 3):
             NX[c, j - 1] = encode(rows_for(c, (zh + j) % 4), UP_IG)
             send((f"N{j}", c), NX.at[c, j - 1], ZX.at[c, j - 1], zmate[j])
@@ -312,12 +290,9 @@
     stages = dict(A=A, D=D, E=E, e=e, G=G, H=H, I=I, k=k, K=K, L=L, N=N, O=O)
     for j in (1, 2, 3):
         stages[f"B{j}"] = lambda c, u, j=j: B(j, c)
-    for j in range(4):
-        stages[f"C{j}"] = lambda c, u, j=j: C(j, c)
     for d in range(2):
         stages[f"F{d}"] = lambda c, u, d=d: F(d, c, u)
         stages[f"J{d}"] = lambda c, u, d=d: J(d, c, u)
-        stages[f"M{d}"] = lambda c, u, d=d: M(d, c)
 
     theirs, ours = pl.multiple_of((1 - core) * 1024, 1024), pl.multiple_of(core * 1024, 1024)
     own = [
@@ -341,15 +316,17 @@
 def local(inputs, out_grad, w_in, w_out):
     vmem = pl.BlockSpec(memory_space=pltpu.VMEM)
     hbm = pl.BlockSpec(memory_space=pl.ANY)
-    input_grad, xg, acts = pl.pallas_call(
+    input_grad, xg, gg, act, pre_grad = pl.pallas_call(
         kernel,
         out_shape=(
             jax.ShapeDtypeStruct((64, 512), F32),
-            jax.ShapeDtypeStruct((2, NC, 16, 16, 512), BF16),
-            jax.ShapeDtypeStruct((2, NC, 4, 2, 32, 2048), BF16),
+            jax.ShapeDtypeStruct((NC, 16, 16, 512), BF16),
+            jax.ShapeDtypeStruct((NC, 16, 16, 512), BF16),
+            jax.ShapeDtypeStruct((NC, 4, 2, 32, 2048), BF16),
+            jax.ShapeDtypeStruct((NC, 4, 2, 32, 2048), BF16),
         ),
         in_specs=[vmem, vmem, hbm, hbm],
-        out_specs=(vmem, hbm, hbm),
+        out_specs=(vmem, hbm, hbm, hbm, hbm),
         scratch_shapes=[
             pltpu.VMEM((NC, 2, 2, 16, 16, 512), BF16),
             pltpu.VMEM((512, 2048), BF16),
@@ -362,8 +339,8 @@
             pltpu.VMEM((NC, Q, 2, 4, 32, 512), BF16),
             pltpu.VMEM((NC, 2, 2, Q, 4, 2, 32, 512), BF16),
             pltpu.VMEM((NC, 4, 2, 32, 512), F32),
-            pltpu.VMEM((NC, 2, 3, 32, 512), BF16),
-            pltpu.VMEM((NC, 2, 3, 32, 512), BF16),
+            pltpu.VMEM((NC, 3, 2, 32, 512), BF16),
+            pltpu.VMEM((NC, 3, 2, 32, 512), BF16),
             pltpu.VMEM((NC, 3, 16, 512), BF16),
             pltpu.VMEM((NC, 3, 16, 512), BF16),
             pltpu.SemaphoreType.DMA((COPIES,)),
@@ -376,12 +353,30 @@
         ),
         cost_estimate=pl.CostEstimate(flops=6 * 2**30, bytes_accessed=16 * 2**20, transcendentals=0),
     )(inputs, out_grad, w_in, w_out)
-    xg = xg.reshape(2, 1024, 512)
-    acts = acts.reshape(2, 1024, 2048)
-    tn = (((0,), (0,)), ((), ()))
-    w_out_grad = lax.dot_general(acts[0], xg[1], tn, preferred_element_type=F32)
-    w_in_grad = lax.dot_general(xg[0], acts[1], tn, preferred_element_type=F32)
+    w_in_grad, w_out_grad = weight_grads(
+        xg.reshape(1024, 512), gg.reshape(1024, 512), act.reshape(1024, 2048), pre_grad.reshape(1024, 2048)
+    )
     return (input_grad, w_in_grad, w_out_grad)
+
+
+def weight_grads(xg, gg, act, pre_grad):
+    steps = 2
+    width = 2048 // steps
+    whole, columns = pl.BlockSpec((1024, 512), lambda i: (0, 0)), pl.BlockSpec((1024, width), lambda i: (0, i))
+
+    def body(x, g, a, p, w_in_grad, w_out_grad):
+        w_in_grad[...] = lax.dot_general(x[...], p[...], TN, preferred_element_type=F32)
+        w_out_grad[...] = lax.dot_general(a[...], g[...], TN, preferred_element_type=F32)
+
+    return pl.pallas_call(
+        body,
+        grid=(steps,),
+        out_shape=(jax.ShapeDtypeStruct((512, 2048), F32), jax.ShapeDtypeStruct((2048, 512), F32)),
+        in_specs=[whole, whole, columns, columns],
+        out_specs=(pl.BlockSpec((512, width), lambda i: (0, i)), pl.BlockSpec((width, 512), lambda i: (i, 0))),
+        compiler_params=pltpu.CompilerParams(vmem_limit_bytes=60 * 2**20),
+        cost_estimate=pl.CostEstimate(flops=4 * 2**30, bytes_accessed=18 * 2**20, transcendentals=0),
+    )(xg, gg, act, pre_grad)
 
 
 def solution(mesh):

time: 123 us -> 114 us (0.927)
  matrix products: 8.93 us -> 0 us
  Pallas kernels: 106 us -> 112 us
  local copies, waits for them, and re-layouts: 6.38 us -> 0.66 us
    dot_general x2 -> x0, matrix products: 8.93 us -> none  [the longest x1 4.47 us: local(): w_in_grad = lax.dot_general(xg[0], acts[1], tn, preferred_element_type=F32)]
    pallas_call x0 -> x1, Pallas kernels: none -> 8.92 us  [weight_grads(): pl.pallas_call(body, grid=(steps,), out_shape=(jax.ShapeDtypeStruct((512,...]
    slice x2 -> x0, local copies, waits for them, and re-layouts: 5.72 us -> none  [local(): w_out_grad = lax.dot_general(acts[0], xg[1], tn, preferred_element_type=F32)]
    pallas_call x1, Pallas kernels: 106 us -> 103 us  [local(): pl.pallas_call(kernel, out_shape=(jax.ShapeDtypeStruct((64, 512), F32), j...]
where the time goes in v3:
time: 114 us; the launch traced here: 113 us
  Pallas kernels  112 us (98%)
    pallas_call x1, Pallas kernels, local(): pl.pallas_call(kernel, out_shape=(jax.ShapeDtypeStruct((64, 512), F32), j...  103 us
    pallas_call x1, Pallas kernels, weight_grads(): pl.pallas_call(body, grid=(steps,), out_shape=(jax.ShapeDtypeStruct((512,...  8.92 us

profile of v3, /device:TPU:1, one launch (start us, length us, event | category | flops | bytes accessed | tf_op | source)
XLA Modules:
  0.0 113.5 jit_solution(8712064360941965937)
XLA Ops:
  0.6 103.3 %shard_map.67 = (f32[64,512]{1,0:T(8,128)}, bf16[4,16,16,512]{3,2,1,0:T(8,128)(2,1)}, bf16[4,16,16,512]{3,2,1,0:T(8,128)(2,1)}, bf16[4,4,2,32,2048]{4,3,2,1,0:T(8,128)(2,1)}, bf16[4,4,2,32,2048]{4,3,2,1,0:T(8,128)(2,1)}) custom-call(bf16[64,512]{1,0:T(8,128)(2,1)} %x_ref.1, bf16[64,512]{1,0:T(8,128)(2,1)} %g_ref.1, bf16[512,2048]{1,0:T(8,128)(2,1)} %w_in.1, ...), custom_call_target="tpu_custom_call" | custom-call | flops 6442450944 | bytes 16777216 | tf_op jit(solution)/shard_map/pallas_call | solution.py:319
  103.9 0.0 copy-start
  103.9 8.9 %shard_map.68 = (f32[512,2048]{1,0:T(8,128)}, f32[2048,512]{1,0:T(8,128)}) custom-call(bf16[1024,512]{1,0:T(8,128)(2,1)} %bitcast.6, bf16[1024,512]{1,0:T(8,128)(2,1)} %bitcast.7, bf16[1024,2048]{1,0:T(8,128)(2,1)} %bitcast.4, bf16[1024,2048]{1,0:T(8,128)(2,1)} %bitcast.5), custom_call_target="tpu_custom_call" | custom-call | flops 4294967296 | bytes 18874368 | tf_op jit(solution)/shard_map/pallas_call | solution.py:371
  112.8 0.0 copy-done
  112.8 0.7 copy.8
Async XLA Ops:
  103.9 8.9 %copy-start = (f32[64,512]{1,0:T(8,128)S(1)}, f32[64,512]{1,0:T(8,128)}, u32[]{:S(2)}) copy-start(f32[64,512]{1,0:T(8,128)} %get-tuple-element.20) | copy-start | bytes 393220

commit v4 on v3

--- a/solution.py
+++ b/solution.py
@@ -10,31 +10,43 @@
 BF16 = jnp.bfloat16
 NC = 4
 Q = 2
-COPIES = 208
+COPIES = 270
 NT = (((1,), (1,)), ((), ()))
 TN = (((0,), (0,)), ((), ()))
 
-Z_FIRST = ((1, 1), (2, 0), (3, 0),)
-Y_FIRST = ((0, 0), (1, 1), (2, 1),)
+Z_FIRST = ((1, 0), (2, 1), (3, 0),)
+Y_FIRST = ((0, 1), (1, 0), (3, 1),)
 ORDER = (
-    ("A", 0, 0), ("A", 1, 0), ("B1", 0, 0), ("B3", 0, 0), ("B2", 0, 0), ("B1", 1, 0),
-    ("B3", 1, 0), ("B2", 1, 0), ("A", 2, 0), ("D", 0, 0), ("B1", 2, 0), ("E", 0, 0),
-    ("B3", 2, 0), ("D", 1, 0), ("B2", 2, 0), ("A", 3, 0), ("E", 0, 1), ("F0", 0, 0),
-    ("E", 1, 1), ("B1", 3, 0), ("F1", 0, 0), ("B3", 3, 0), ("D", 2, 0), ("B2", 3, 0),
-    ("F1", 0, 1), ("F0", 0, 1), ("E", 1, 0), ("E", 2, 1), ("G", 0, 0), ("E", 2, 0),
-    ("D", 3, 0), ("e", 1, 1), ("G", 0, 1), ("F1", 1, 0), ("F0", 1, 0), ("H", 0, 0),
-    ("E", 3, 1), ("E", 3, 0), ("F1", 2, 1), ("F0", 2, 1), ("F0", 1, 1), ("F1", 1, 1),
-    ("G", 1, 0), ("e", 2, 0), ("J0", 0, 0), ("J1", 0, 0), ("H", 0, 1), ("F0", 3, 1),
-    ("F1", 3, 1), ("G", 2, 1), ("H", 1, 1), ("F0", 2, 0), ("F1", 2, 0), ("e", 3, 0),
-    ("k", 0, 0), ("H", 1, 0), ("G", 3, 1), ("I", 0, 1), ("J0", 1, 1), ("J1", 1, 1),
-    ("H", 2, 1), ("H", 2, 0), ("F0", 3, 0), ("F1", 3, 0), ("J0", 0, 1), ("J1", 0, 1),
-    ("k", 1, 1), ("K", 0, 0), ("J0", 2, 1), ("J1", 2, 1), ("I", 1, 0), ("H", 3, 0),
-    ("L", 0, 0), ("H", 3, 1), ("K", 0, 1), ("k", 2, 1), ("I", 2, 0), ("L", 0, 1),
-    ("J0", 1, 0), ("J1", 1, 0), ("J0", 2, 0), ("J1", 2, 0), ("K", 1, 1), ("K", 1, 0),
-    ("I", 3, 0), ("N", 0, 1), ("I", 3, 1), ("K", 2, 0), ("L", 1, 0), ("L", 1, 1),
-    ("L", 2, 0), ("J0", 3, 0), ("J1", 3, 0), ("K", 2, 1), ("J0", 3, 1), ("J1", 3, 1),
-    ("O", 0, 1), ("N", 1, 1), ("K", 3, 0), ("L", 2, 1), ("K", 3, 1), ("L", 3, 0),
-    ("O", 1, 1), ("L", 3, 1), ("N", 2, 1), ("O", 2, 1), ("N", 3, 1), ("O", 3, 1),
+    ("Ax", 0, 0), ("A", 1, 0), ("A", 3, 0), ("B1x", 0, 0), ("B3x", 0, 0), ("B2x", 0, 0),
+    ("B2", 1, 0), ("B1", 1, 0), ("B3", 1, 0), ("Dx", 0, 0), ("Ag", 0, 0), ("B1", 3, 0),
+    ("B2", 3, 0), ("Ex", 0, 1), ("Ex", 0, 0), ("B3", 3, 0), ("A", 2, 0), ("D", 1, 0),
+    ("F0x", 0, 1), ("F1x", 0, 1), ("B1g", 0, 0), ("E", 1, 1), ("E", 1, 0), ("F0x", 0, 0),
+    ("B3g", 0, 0), ("B2g", 0, 0), ("B2", 2, 0), ("D", 3, 0), ("B3", 2, 0), ("F1x", 0, 0),
+    ("F1", 1, 1), ("F0", 1, 1), ("E", 3, 1), ("B1", 2, 0), ("Dg", 0, 0), ("E", 3, 0),
+    ("Eg", 0, 0), ("Eg", 0, 1), ("e", 1, 0), ("D", 2, 0), ("F0", 3, 1), ("F1g", 0, 0),
+    ("F1", 3, 1), ("E", 2, 1), ("F1g", 0, 1), ("F0g", 0, 0), ("G", 1, 1), ("F0g", 0, 1),
+    ("F0", 1, 0), ("F1", 1, 0), ("E", 2, 0), ("e", 3, 0), ("H", 1, 0), ("G", 0, 0),
+    ("Sp", 1, 0), ("Sa", 1, 0), ("G", 3, 1), ("e", 2, 1), ("F0", 2, 0), ("G", 0, 1),
+    ("F1", 2, 0), ("H", 1, 1), ("H", 0, 0), ("Sp", 1, 1), ("J0p", 1, 0), ("J1p", 1, 0),
+    ("Sa", 0, 0), ("Sp", 0, 0), ("F1", 3, 0), ("Sa", 1, 1), ("F0", 2, 1), ("H", 3, 1),
+    ("Sp", 3, 1), ("F1", 2, 1), ("Sa", 3, 1), ("F0", 3, 0), ("G", 2, 0), ("H", 0, 1),
+    ("Ip", 1, 1), ("Sp", 0, 1), ("kp", 1, 0), ("Ip", 0, 0), ("H", 3, 0), ("J0a", 3, 1),
+    ("H", 2, 0), ("J1a", 1, 0), ("Sp", 3, 0), ("Sp", 2, 0), ("J0p", 3, 1), ("J0a", 1, 0),
+    ("J1p", 1, 1), ("H", 2, 1), ("J0p", 0, 1), ("J1p", 0, 1), ("Sp", 2, 1), ("J1p", 3, 1),
+    ("Sa", 3, 0), ("J0p", 1, 1), ("Sa", 2, 0), ("J1a", 3, 1), ("J0p", 0, 0), ("J1p", 0, 0),
+    ("Ip", 3, 0), ("kp", 0, 1), ("Ip", 2, 0), ("Ip", 2, 1), ("Sa", 0, 1), ("kp", 3, 1),
+    ("Kp", 1, 0), ("Kp", 1, 1), ("L", 1, 0), ("Kp", 0, 0), ("L", 1, 1), ("Sa", 2, 1),
+    ("J1p", 3, 0), ("J0p", 2, 0), ("J1p", 2, 0), ("J0p", 3, 0), ("Kp", 0, 1), ("J0p", 2, 1),
+    ("J1p", 2, 1), ("ka", 3, 1), ("L", 0, 0), ("L", 0, 1), ("J1a", 0, 1), ("Ia", 3, 0),
+    ("J0a", 0, 1), ("ka", 1, 0), ("Kp", 2, 0), ("Ia", 0, 0), ("Ia", 2, 0), ("Kp", 3, 0),
+    ("Kp", 2, 1), ("Kp", 3, 1), ("Ia", 2, 1), ("L", 2, 0), ("L", 2, 1), ("N", 1, 1),
+    ("Ia", 1, 1), ("L", 3, 0), ("ka", 0, 1), ("N", 0, 1), ("J1a", 3, 0), ("J0a", 3, 0),
+    ("L", 3, 1), ("J0a", 2, 0), ("N", 2, 1), ("J0a", 2, 1), ("Ka", 1, 0), ("J0a", 0, 0),
+    ("J1a", 2, 0), ("J0a", 1, 1), ("J1a", 0, 0), ("J1a", 1, 1), ("J1a", 2, 1), ("Ka", 3, 1),
+    ("N", 3, 1), ("Q", 1, 0), ("Ka", 3, 0), ("Ka", 2, 0), ("Ka", 0, 1), ("Q", 3, 1),
+    ("Ka", 1, 1), ("O", 1, 1), ("Ka", 0, 0), ("Q", 3, 0), ("Ka", 2, 1), ("O", 2, 1),
+    ("Q", 2, 0), ("O", 0, 1), ("Q", 0, 0), ("Q", 1, 1), ("Q", 0, 1), ("Q", 2, 1),
+    ("O", 3, 1),
 )
 
 
@@ -100,65 +112,74 @@
         copy.start()
         locals_.append(copy)
 
-    def A(c, u):
+    arrays = {"": (0, 1), "x": (0,), "g": (1,)}
+    span = {"": slice(None), "x": pl.ds(0, 1), "g": pl.ds(1, 1)}
+
+    def versions(c):
+        return ("x", "g") if c == 0 else ("",)
+
+    def A(c, u, v):
         rows = pl.ds(16 * c, 16)
-        XG[c, 0, core, h] = x_ref[rows, :]
-        XG[c, 1, core, h] = g_ref[rows, :]
-        mine = XG.at[c, :, core, h]
-        for j in (1, 3, 2):
-            send((f"A{j}", c), mine, mine, zmate[j])
-        across(0, c)
-
-    def across(j, c):
-        block = XG.at[c, :, core, 4 * x + behind[j]]
-        for i in (1, 3, 2):
-            send((f"B{j}{i}", c), block, block, xmate[i])
-
-    def B(j, c):
-        arrived((f"A{j}", c))
-        across(j, c)
-
-    def D(c, u):
-        arrived(*((f"B{j}{i}", c) for j in range(4) for i in (1, 2, 3)))
-        mine = XG.at[c, :, core]
-        send(("D", c), mine, mine, partner)
-        keep(XG.at[c, 0, core], xo.at[c])
-        keep(XG.at[c, 1, core], go.at[c])
+        for a in arrays[v]:
+            XG[c, a, core, h] = (x_ref, g_ref)[a][rows, :]
+        mine = XG.at[c, span[v], core, h]
+        for j in (2, 1, 3):
+            send((f"A{j}{v}", c), mine, mine, zmate[j])
+        across(0, c, v)
+
+    def across(j, c, v):
+        block = XG.at[c, span[v], core, 4 * x + behind[j]]
+        for i in (2, 1, 3):
+            send((f"B{j}{i}{v}", c), block, block, xmate[i])
+
+    def B(j, c, v):
+        arrived((f"A{j}{v}", c))
+        across(j, c, v)
+
+    def D(c, u, v):
+        arrived(*((f"B{j}{i}{v}", c) for j in range(4) for i in (1, 2, 3)))
+        mine = XG.at[c, span[v], core]
+        send((f"D{v}", c), mine, mine, partner)
+        for a in arrays[v]:
+            keep(XG.at[c, a, core], (xo, go)[a].at[c])
 
     ready = []
 
-    def E(c, u):
-        if not ready:
-            arrived("w_in", "w_out")
-            for copy in own:
-                copy.wait()
-        if ("D", c) not in ready:
-            arrived(("D", c))
-        ready.append(("D", c))
+    def once(key, wait):
+        if key not in ready:
+            wait()
+        ready.append(key)
+
+    def E(c, u, v):
+        for a in arrays[v]:
+            once(("w", a), lambda a=a: (arrived(("w_in", "w_out")[a]), own[a].wait()))
+        once(("D", c, v), lambda: arrived((f"D{v}", c)))
 
         @pl.loop(0, 2)
         def _(n):
             cols = pl.ds(pl.multiple_of(n * 256, 256), 256)
             wide = pl.ds(pl.multiple_of(n * 256 + 512 * u, 256), 256)
-            pre = jnp.dot(XG[c, 0, 0].reshape(256, 512), W1[0, :, wide], preferred_element_type=F32)
-            pre += jnp.dot(XG[c, 0, 1].reshape(256, 512), W1[1, :, wide], preferred_element_type=F32)
-            PT[c, u, 0, :, :, :, cols] = pre.reshape(4, 2, 32, 256)
-            hid = lax.dot_general(XG[c, 1, 0].reshape(256, 512), W2[0, wide, :], NT, preferred_element_type=F32)
-            hid += lax.dot_general(XG[c, 1, 1].reshape(256, 512), W2[1, wide, :], NT, preferred_element_type=F32)
-            PT[c, u, 1, :, :, :, cols] = hid.reshape(4, 2, 32, 256)
+            if 0 in arrays[v]:
+                pre = jnp.dot(XG[c, 0, 0].reshape(256, 512), W1[0, :, wide], preferred_element_type=F32)
+                pre += jnp.dot(XG[c, 0, 1].reshape(256, 512), W1[1, :, wide], preferred_element_type=F32)
+                PT[c, u, 0, :, :, :, cols] = pre.reshape(4, 2, 32, 256)
+            if 1 in arrays[v]:
+                hid = lax.dot_general(XG[c, 1, 0].reshape(256, 512), W2[0, wide, :], NT, preferred_element_type=F32)
+                hid += lax.dot_general(XG[c, 1, 1].reshape(256, 512), W2[1, wide, :], NT, preferred_element_type=F32)
+                PT[c, u, 1, :, :, :, cols] = hid.reshape(4, 2, 32, 256)
 
         if (c, u) in Z_FIRST:
             for a in range(2):
                 ZT[c, u, a] = encode(PT[c, u, a, :, 1 - zl])
             send(("z", c, u), ZT.at[c, u], ZR.at[c, u], zpair)
         else:
-            tree(c, u)
+            tree(c, u, v)
 
     def e(c, u):
         arrived(("z", c, u))
         for a in range(2):
             PT[c, u, a, :, zl] = PT[c, u, a, :, zl] + decode(ZR[c, u, a])
-        tree(c, u)
+        tree(c, u, "")
 
     def part(c, u, a, piece, half):
         if (c, u) in Z_FIRST:
@@ -168,22 +189,25 @@
     def rows_of(c, u):
         return pl.ds(0, 16 if (c, u) in Z_FIRST else 32)
 
-    def tree(c, u):
+    def tree(c, u, v):
         rows = rows_of(c, u)
         for d, kind, piece, half, to in (
             (0, 0, yf, 0, right), (1, 0, yf, 1, left), (0, 1, yr, 1, right), (1, 1, yl, 0, left),
         ):
-            for a in range(2):
+            for a in arrays[v]:
                 TX[c, u, d, kind, a, rows] = encode(part(c, u, a, piece, half)[...])
-            send((f"y{d}{kind}", c, u), TX.at[c, u, d, kind, :, rows], RX.at[c, u, d, kind, :, rows], to)
-
-    def F(d, c, u):
+            send((f"y{d}{kind}{v}", c, u), TX.at[c, u, d, kind, span[v], rows], RX.at[c, u, d, kind, span[v], rows], to)
+
+    def F(d, c, u, v):
         rows = rows_of(c, u)
         piece, half, to = ((yr, 0, right), (yl, 1, left))[d]
-        arrived((f"y{d}0", c, u))
-        for a in range(2):
+        arrived((f"y{d}0{v}", c, u))
+        for a in arrays[v]:
             TX[c, u, d, 2, a, rows] = encode(part(c, u, a, piece, half)[...] + decode(RX[c, u, d, 0, a, rows]))
-        send((f"y{d}2", c, u), TX.at[c, u, d, 2, :, rows], RX.at[c, u, d, 2, :, rows], to)
+        send((f"y{d}2{v}", c, u), TX.at[c, u, d, 2, span[v], rows], RX.at[c, u, d, 2, span[v], rows], to)
+
+    def sums(c, u):
+        arrived(*((f"y{d}{kind}{v}", c, u) for d in range(2) for kind in (1, 2) for v in versions(c)))
 
     def own_sum(c, u, a, half):
         rows = rows_of(c, u)
@@ -194,7 +218,7 @@
         )
 
     def G(c, u):
-        arrived(*((f"y{d}{kind}", c, u) for d in range(2) for kind in (1, 2)))
+        sums(c, u)
         for a in range(2):
             ZT[c, u, a, 0] = encode(own_sum(c, u, a, 1 - zl))
         send(("z", c, u), ZT.at[c, u, :, 0], ZR.at[c, u, :, 0], zpair)
@@ -203,7 +227,7 @@
 
     def H(c, u):
         if (c, u) in Z_FIRST:
-            arrived(*((f"y{d}{kind}", c, u) for d in range(2) for kind in (1, 2)))
+            sums(c, u)
             for half in range(2):
                 rows = pl.ds(16 * half, 16)
                 value, slope = gelu_parts(own_sum(c, u, 0, half))
@@ -215,43 +239,48 @@
             hidden = PT[c, u, 1, y, zl] + decode(ZR[c, u, 1, 0])
             ACT[c, 0, core, u, y, zl] = value.astype(BF16)
             ACT[c, 1, core, u, y, zl] = (hidden * slope).astype(BF16)
-        mine = ACT.at[c, :, core, u, y, zl]
+
+    def S(a, c, u):
+        mine = ACT.at[c, a, core, u, y, zl]
         if (c, u) in Y_FIRST:
-            send(("I0", c, u), mine, mine, right)
-            send(("I1", c, u), mine, mine, left)
+            send(("I0", a, c, u), mine, mine, right)
+            send(("I1", a, c, u), mine, mine, left)
         else:
-            send(("H", c, u), mine, mine, zpair)
-
-    def I(c, u):
-        arrived(("H", c, u))
-        mine = ACT.at[c, :, core, u, y]
-        send(("I0", c, u), mine, mine, right)
-        send(("I1", c, u), mine, mine, left)
-
-    def J(d, c, u):
-        arrived((f"I{d}", c, u))
+            send(("S", a, c, u), mine, mine, zpair)
+
+    def I(a, c, u):
+        arrived(("S", a, c, u))
+        mine = ACT.at[c, a, core, u, y]
+        send(("I0", a, c, u), mine, mine, right)
+        send(("I1", a, c, u), mine, mine, left)
+
+    def J(d, a, c, u):
+        arrived((f"I{d}", a, c, u))
         piece, to = ((yl, right), (yr, left))[d]
         if (c, u) in Y_FIRST:
-            block = ACT.at[c, :, core, u, piece, zl, pl.ds(16 * d, 16)]
+            block = ACT.at[c, a, core, u, piece, zl, pl.ds(16 * d, 16)]
         else:
-            block = ACT.at[c, :, core, u, piece, d]
-        send((f"J{d}", c, u), block, block, to)
-
-    def k(c, u):
-        arrived(("J0", c, u), ("J1", c, u))
-        mine = ACT.at[c, :, core, u, :, zl]
-        send(("k", c, u), mine, mine, zpair)
-
-    def K(c, u):
-        arrived(*([("k", c, u)] if (c, u) in Y_FIRST else [("J0", c, u), ("J1", c, u)]))
-        mine = ACT.at[c, :, core, u]
-        send(("K", c, u), mine, mine, partner)
+            block = ACT.at[c, a, core, u, piece, d]
+        send((f"J{d}", a, c, u), block, block, to)
+
+    def k(a, c, u):
+        arrived(("J0", a, c, u), ("J1", a, c, u))
+        mine = ACT.at[c, a, core, u, :, zl]
+        send(("k", a, c, u), mine, mine, zpair)
+
+    def K(a, c, u):
+        arrived(*([("k", a, c, u)] if (c, u) in Y_FIRST else [("J0", a, c, u), ("J1", a, c, u)]))
+        mine = ACT.at[c, a, core, u]
+        send(("K", a, c, u), mine, mine, partner)
+
+    def whole(a, c, u):
+        arrived(("K", a, c, u))
+        for half in range(2):
+            keep(ACT.at[c, a, half, u], (ao, po)[a].at[c, :, :, :, pl.ds(1024 * half + 512 * u, 512)])
 
     def L(c, u):
-        arrived(("K", c, u))
-        for a in range(2):
-            for half in range(2):
-                keep(ACT.at[c, a, half, u], (ao, po)[a].at[c, :, :, :, pl.ds(1024 * half + 512 * u, 512)])
+        whole(1, c, u)
+        once(("w", 2), own[2].wait)
 
         @pl.loop(0, 2)
         def _(n):
@@ -267,7 +296,7 @@
 
         if u == 0:
             return
-        for j in (1, 3, 2):
+        for j in (2, 1, 3):
             XT[c, j - 1] = encode(IGP[c, (x + j) % 4], UP_IG)
             send((f"x{j}", c), XT.at[c, j - 1], XR.at[c, j - 1], xmate[j])
 
@@ -275,7 +304,7 @@
         arrived(("x1", c), ("x2", c), ("x3", c))
         others = decode(XR[c, 0], DOWN_IG) + decode(XR[c, 1], DOWN_IG) + decode(XR[c, 2], DOWN_IG)
         IGP[c, x] = IGP[c, x] + others
-        for j in (1, 2, 3):
+        for j in (2, 1, 3):
             NX[c, j - 1] = encode(rows_for(c, (zh + j) % 4), UP_IG)
             send((f"N{j}", c), NX.at[c, j - 1], ZX.at[c, j - 1], zmate[j])
 
@@ -287,12 +316,19 @@
         others = decode(ZX[c, 0], DOWN_IG) + decode(ZX[c, 1], DOWN_IG) + decode(ZX[c, 2], DOWN_IG)
         ig_ref[pl.ds(16 * c, 16), :] = rows_for(c, zh) + others
 
-    stages = dict(A=A, D=D, E=E, e=e, G=G, H=H, I=I, k=k, K=K, L=L, N=N, O=O)
-    for j in (1, 2, 3):
-        stages[f"B{j}"] = lambda c, u, j=j: B(j, c)
-    for d in range(2):
-        stages[f"F{d}"] = lambda c, u, d=d: F(d, c, u)
-        stages[f"J{d}"] = lambda c, u, d=d: J(d, c, u)
+    stages = dict(e=e, G=G, H=H, L=L, N=N, O=O, Q=lambda c, u: whole(0, c, u))
+    for v in ("", "x", "g"):
+        for name, f in (("A", A), ("D", D), ("E", E)):
+            stages[name + v] = lambda c, u, f=f, v=v: f(c, u, v)
+        for j in (1, 2, 3):
+            stages[f"B{j}{v}"] = lambda c, u, j=j, v=v: B(j, c, v)
+        for d in range(2):
+            stages[f"F{d}{v}"] = lambda c, u, d=d, v=v: F(d, c, u, v)
+    for a, v in enumerate("ap"):
+        for name, f in (("S", S), ("I", I), ("k", k), ("K", K)):
+            stages[name + v] = lambda c, u, a=a, f=f: f(a, c, u)
+        for d in range(2):
+            stages[f"J{d}{v}"] = lambda c, u, d=d, a=a: J(d, a, c, u)
 
     theirs, ours = pl.multiple_of((1 - core) * 1024, 1024), pl.multiple_of(core * 1024, 1024)
     own = [

time: 114 us -> 104 us (0.912)
  Pallas kernels: 112 us -> 102 us
    pallas_call x1, Pallas kernels: 103 us -> 93.4 us  [local(): pl.pallas_call(kernel, out_shape=(jax.ShapeDtypeStruct((64, 512), F32), j...]
where the time goes in v4:
time: 104 us
  Pallas kernels  102 us (98%)
    pallas_call x1, Pallas kernels, local(): pl.pallas_call(kernel, out_shape=(jax.ShapeDtypeStruct((64, 512), F32), j...  93.4 us
    pallas_call x1, Pallas kernels, weight_grads(): pl.pallas_call(body, grid=(steps,), out_shape=(jax.ShapeDtypeStruct((512,...  8.92 us

profile of v4, /device:TPU:1, one launch (start us, length us, event | category | flops | bytes accessed | tf_op | source)
XLA Modules:
  0.0 103.6 jit_solution(1249331341699365593)
XLA Ops:
  0.6 93.4 %shard_map.67 = (f32[64,512]{1,0:T(8,128)}, bf16[4,16,16,512]{3,2,1,0:T(8,128)(2,1)}, bf16[4,16,16,512]{3,2,1,0:T(8,128)(2,1)}, bf16[4,4,2,32,2048]{4,3,2,1,0:T(8,128)(2,1)}, bf16[4,4,2,32,2048]{4,3,2,1,0:T(8,128)(2,1)}) custom-call(bf16[64,512]{1,0:T(8,128)(2,1)} %x_ref.1, bf16[64,512]{1,0:T(8,128)(2,1)} %g_ref.1, bf16[512,2048]{1,0:T(8,128)(2,1)} %w_in.1, ...), custom_call_target="tpu_custom_call" | custom-call | flops 6442450944 | bytes 16777216 | tf_op jit(solution)/shard_map/pallas_call | solution.py:355
  94.0 0.0 copy-start
  94.0 8.9 %shard_map.68 = (f32[512,2048]{1,0:T(8,128)}, f32[2048,512]{1,0:T(8,128)}) custom-call(bf16[1024,512]{1,0:T(8,128)(2,1)} %bitcast.6, bf16[1024,512]{1,0:T(8,128)(2,1)} %bitcast.7, bf16[1024,2048]{1,0:T(8,128)(2,1)} %bitcast.4, bf16[1024,2048]{1,0:T(8,128)(2,1)} %bitcast.5), custom_call_target="tpu_custom_call" | custom-call | flops 4294967296 | bytes 18874368 | tf_op jit(solution)/shard_map/pallas_call | solution.py:407
  103.0 0.0 copy-done
  103.0 0.7 copy.8
Async XLA Ops:
  94.0 8.9 %copy-start = (f32[64,512]{1,0:T(8,128)S(1)}, f32[64,512]{1,0:T(8,128)}, u32[]{:S(2)}) copy-start(f32[64,512]{1,0:T(8,128)} %get-tuple-element.20) | copy-start | bytes 393220

commit v5 on v4

--- a/solution.py
+++ b/solution.py
@@ -14,38 +14,38 @@
 NT = (((1,), (1,)), ((), ()))
 TN = (((0,), (0,)), ((), ()))
 
-Z_FIRST = ((1, 0), (2, 1), (3, 0),)
-Y_FIRST = ((0, 1), (1, 0), (3, 1),)
+Z_FIRST = ((1, 0), (3, 1),)
+Y_FIRST = ((0, 0), (1, 0), (1, 1),)
 ORDER = (
-    ("Ax", 0, 0), ("A", 1, 0), ("A", 3, 0), ("B1x", 0, 0), ("B3x", 0, 0), ("B2x", 0, 0),
-    ("B2", 1, 0), ("B1", 1, 0), ("B3", 1, 0), ("Dx", 0, 0), ("Ag", 0, 0), ("B1", 3, 0),
-    ("B2", 3, 0), ("Ex", 0, 1), ("Ex", 0, 0), ("B3", 3, 0), ("A", 2, 0), ("D", 1, 0),
-    ("F0x", 0, 1), ("F1x", 0, 1), ("B1g", 0, 0), ("E", 1, 1), ("E", 1, 0), ("F0x", 0, 0),
-    ("B3g", 0, 0), ("B2g", 0, 0), ("B2", 2, 0), ("D", 3, 0), ("B3", 2, 0), ("F1x", 0, 0),
-    ("F1", 1, 1), ("F0", 1, 1), ("E", 3, 1), ("B1", 2, 0), ("Dg", 0, 0), ("E", 3, 0),
-    ("Eg", 0, 0), ("Eg", 0, 1), ("e", 1, 0), ("D", 2, 0), ("F0", 3, 1), ("F1g", 0, 0),
-    ("F1", 3, 1), ("E", 2, 1), ("F1g", 0, 1), ("F0g", 0, 0), ("G", 1, 1), ("F0g", 0, 1),
-    ("F0", 1, 0), ("F1", 1, 0), ("E", 2, 0), ("e", 3, 0), ("H", 1, 0), ("G", 0, 0),
-    ("Sp", 1, 0), ("Sa", 1, 0), ("G", 3, 1), ("e", 2, 1), ("F0", 2, 0), ("G", 0, 1),
-    ("F1", 2, 0), ("H", 1, 1), ("H", 0, 0), ("Sp", 1, 1), ("J0p", 1, 0), ("J1p", 1, 0),
-    ("Sa", 0, 0), ("Sp", 0, 0), ("F1", 3, 0), ("Sa", 1, 1), ("F0", 2, 1), ("H", 3, 1),
-    ("Sp", 3, 1), ("F1", 2, 1), ("Sa", 3, 1), ("F0", 3, 0), ("G", 2, 0), ("H", 0, 1),
-    ("Ip", 1, 1), ("Sp", 0, 1), ("kp", 1, 0), ("Ip", 0, 0), ("H", 3, 0), ("J0a", 3, 1),
-    ("H", 2, 0), ("J1a", 1, 0), ("Sp", 3, 0), ("Sp", 2, 0), ("J0p", 3, 1), ("J0a", 1, 0),
-    ("J1p", 1, 1), ("H", 2, 1), ("J0p", 0, 1), ("J1p", 0, 1), ("Sp", 2, 1), ("J1p", 3, 1),
-    ("Sa", 3, 0), ("J0p", 1, 1), ("Sa", 2, 0), ("J1a", 3, 1), ("J0p", 0, 0), ("J1p", 0, 0),
-    ("Ip", 3, 0), ("kp", 0, 1), ("Ip", 2, 0), ("Ip", 2, 1), ("Sa", 0, 1), ("kp", 3, 1),
-    ("Kp", 1, 0), ("Kp", 1, 1), ("L", 1, 0), ("Kp", 0, 0), ("L", 1, 1), ("Sa", 2, 1),
-    ("J1p", 3, 0), ("J0p", 2, 0), ("J1p", 2, 0), ("J0p", 3, 0), ("Kp", 0, 1), ("J0p", 2, 1),
-    ("J1p", 2, 1), ("ka", 3, 1), ("L", 0, 0), ("L", 0, 1), ("J1a", 0, 1), ("Ia", 3, 0),
-    ("J0a", 0, 1), ("ka", 1, 0), ("Kp", 2, 0), ("Ia", 0, 0), ("Ia", 2, 0), ("Kp", 3, 0),
-    ("Kp", 2, 1), ("Kp", 3, 1), ("Ia", 2, 1), ("L", 2, 0), ("L", 2, 1), ("N", 1, 1),
-    ("Ia", 1, 1), ("L", 3, 0), ("ka", 0, 1), ("N", 0, 1), ("J1a", 3, 0), ("J0a", 3, 0),
-    ("L", 3, 1), ("J0a", 2, 0), ("N", 2, 1), ("J0a", 2, 1), ("Ka", 1, 0), ("J0a", 0, 0),
-    ("J1a", 2, 0), ("J0a", 1, 1), ("J1a", 0, 0), ("J1a", 1, 1), ("J1a", 2, 1), ("Ka", 3, 1),
-    ("N", 3, 1), ("Q", 1, 0), ("Ka", 3, 0), ("Ka", 2, 0), ("Ka", 0, 1), ("Q", 3, 1),
-    ("Ka", 1, 1), ("O", 1, 1), ("Ka", 0, 0), ("Q", 3, 0), ("Ka", 2, 1), ("O", 2, 1),
-    ("Q", 2, 0), ("O", 0, 1), ("Q", 0, 0), ("Q", 1, 1), ("Q", 0, 1), ("Q", 2, 1),
+    ("Ax", 0, 0), ("Ag", 0, 0), ("A", 1, 0), ("A", 2, 0), ("B1x", 0, 0), ("B2x", 0, 0),
+    ("B3x", 0, 0), ("B2g", 0, 0), ("B3g", 0, 0), ("B1g", 0, 0), ("B2", 1, 0), ("B3", 1, 0),
+    ("B1", 1, 0), ("Dx", 0, 0), ("A", 3, 0), ("Ex", 0, 1), ("Dg", 0, 0), ("Ex", 0, 0),
+    ("B2", 2, 0), ("B3", 2, 0), ("Eg", 0, 0), ("Eg", 0, 1), ("D", 1, 0), ("F0x", 0, 1),
+    ("B1", 2, 0), ("F0x", 0, 0), ("B1", 3, 0), ("F1x", 0, 1), ("B2", 3, 0), ("F1x", 0, 0),
+    ("E", 1, 1), ("B3", 3, 0), ("F1g", 0, 0), ("E", 1, 0), ("F1g", 0, 1), ("D", 2, 0),
+    ("F0g", 0, 0), ("F0g", 0, 1), ("F0", 1, 1), ("F1", 1, 1), ("E", 2, 1), ("D", 3, 0),
+    ("G", 0, 0), ("E", 2, 0), ("G", 0, 1), ("E", 3, 1), ("F1", 2, 1), ("F0", 2, 1),
+    ("e", 1, 0), ("H", 0, 0), ("F1", 2, 0), ("Sp", 0, 0), ("F0", 2, 0), ("G", 1, 1),
+    ("E", 3, 0), ("F0", 1, 0), ("G", 2, 1), ("F1", 1, 0), ("e", 3, 1), ("G", 2, 0),
+    ("H", 0, 1), ("Sp", 0, 1), ("F0", 3, 0), ("F1", 3, 0), ("J1p", 0, 0), ("H", 1, 1),
+    ("J0p", 0, 0), ("Sa", 0, 1), ("Sp", 1, 1), ("H", 2, 1), ("H", 1, 0), ("Sp", 1, 0),
+    ("Sp", 2, 1), ("H", 2, 0), ("Sp", 2, 0), ("F0", 3, 1), ("Sa", 1, 1), ("Sa", 2, 1),
+    ("F1", 3, 1), ("Ip", 0, 1), ("G", 3, 0), ("kp", 0, 0), ("J1p", 1, 0), ("J0p", 1, 0),
+    ("J1p", 1, 1), ("Ip", 2, 1), ("H", 3, 1), ("J0p", 1, 1), ("Sp", 3, 1), ("Sa", 1, 0),
+    ("H", 3, 0), ("Sp", 3, 0), ("J0p", 0, 1), ("Ip", 2, 0), ("J0a", 1, 1), ("J1a", 1, 1),
+    ("kp", 1, 0), ("J1p", 0, 1), ("kp", 1, 1), ("Kp", 0, 0), ("Sa", 0, 0), ("J0p", 2, 1),
+    ("J1a", 1, 0), ("J0a", 1, 0), ("Sa", 3, 1), ("Sa", 3, 0), ("Sa", 2, 0), ("Ip", 3, 0),
+    ("Ip", 3, 1), ("ka", 1, 1), ("J1p", 2, 0), ("Kp", 0, 1), ("J0p", 2, 0), ("L", 0, 0),
+    ("J1p", 2, 1), ("Kp", 1, 0), ("J0a", 0, 0), ("Ia", 0, 1), ("L", 0, 1), ("J1p", 3, 0),
+    ("J1a", 0, 0), ("J0p", 3, 0), ("Kp", 1, 1), ("L", 1, 0), ("J1p", 3, 1), ("J0p", 3, 1),
+    ("Kp", 2, 1), ("Kp", 2, 0), ("L", 1, 1), ("Ia", 3, 0), ("Ia", 2, 0), ("ka", 1, 0),
+    ("L", 2, 0), ("Kp", 3, 0), ("L", 2, 1), ("Kp", 3, 1), ("ka", 0, 0), ("Ia", 2, 1),
+    ("L", 3, 0), ("Ia", 3, 1), ("L", 3, 1), ("N", 1, 1), ("N", 0, 1), ("Ka", 1, 1),
+    ("J0a", 0, 1), ("J1a", 3, 0), ("J1a", 2, 1), ("J1a", 2, 0), ("J0a", 2, 0), ("J0a", 2, 1),
+    ("N", 2, 1), ("Ka", 0, 0), ("J0a", 3, 1), ("J1a", 0, 1), ("J0a", 3, 0), ("J1a", 3, 1),
+    ("N", 3, 1), ("Ka", 1, 0), ("Ka", 2, 0), ("Ka", 2, 1), ("O", 0, 1), ("Ka", 0, 1),
+    ("Ka", 3, 0), ("Q", 1, 0), ("Ka", 3, 1), ("Q", 2, 1), ("O", 2, 1), ("Q", 0, 0),
+    ("Q", 1, 1), ("Q", 0, 1), ("O", 1, 1), ("Q", 2, 0), ("Q", 3, 0), ("Q", 3, 1),
     ("O", 3, 1),
 )
 
@@ -85,6 +85,22 @@
     xmate = {j: dev(x=(x + j) % 4) for j in (1, 2, 3)}
     zmate = {j: dev(zh=(zh + j) % 4) for j in (1, 2, 3)}
     behind = {j: (zh + 4 - j) % 4 for j in (0, 1, 2, 3)}
+
+    theirs, ours = pl.multiple_of((1 - core) * 1024, 1024), pl.multiple_of(core * 1024, 1024)
+    mine_in = {}
+    for c in range(NC):
+        for a in range(2):
+            mine_in[c, a] = pltpu.make_async_copy(
+                (x_ref, g_ref)[a].at[pl.ds(16 * c, 16), :], XG.at[c, a, core, h], wsem.at[3 + 2 * c + a]
+            )
+            mine_in[c, a].start()
+    own = [
+        pltpu.make_async_copy(w_in.at[:, pl.ds(ours, 1024)], W1.at[core], wsem.at[0]),
+        pltpu.make_async_copy(w_out.at[pl.ds(ours, 1024), :], W2.at[core], wsem.at[1]),
+        pltpu.make_async_copy(w_in, WV, wsem.at[2]),
+    ]
+    for copy in own:
+        copy.start()
 
     barrier = pltpu.get_barrier_semaphore()
     others = [right, left, partner, zpair, *xmate.values(), *zmate.values()]
@@ -119,9 +135,8 @@
         return ("x", "g") if c == 0 else ("",)
 
     def A(c, u, v):
-        rows = pl.ds(16 * c, 16)
         for a in arrays[v]:
-            XG[c, a, core, h] = (x_ref, g_ref)[a][rows, :]
+            mine_in[c, a].wait()
         mine = XG.at[c, span[v], core, h]
         for j in (2, 1, 3):
             send((f"A{j}{v}", c), mine, mine, zmate[j])
@@ -330,19 +345,11 @@
         for d in range(2):
             stages[f"J{d}{v}"] = lambda c, u, d=d, a=a: J(d, a, c, u)
 
-    theirs, ours = pl.multiple_of((1 - core) * 1024, 1024), pl.multiple_of(core * 1024, 1024)
-    own = [
-        pltpu.make_async_copy(w_in.at[:, pl.ds(ours, 1024)], W1.at[core], wsem.at[0]),
-        pltpu.make_async_copy(w_out.at[pl.ds(ours, 1024), :], W2.at[core], wsem.at[1]),
-        pltpu.make_async_copy(w_in, WV, wsem.at[2]),
-    ]
     for i, (stage, c, u) in enumerate(ORDER):
         stages[stage](c, u)
         if i == 0:
             send("w_in", w_in.at[:, pl.ds(theirs, 1024)], W1.at[core], partner)
             send("w_out", w_out.at[pl.ds(theirs, 1024), :], W2.at[core], partner)
-            for copy in own:
-                copy.start()
     for copy in copies.values():
         copy.wait_send()
     for copy in locals_:
@@ -361,7 +368,7 @@
             jax.ShapeDtypeStruct((NC, 4, 2, 32, 2048), BF16),
             jax.ShapeDtypeStruct((NC, 4, 2, 32, 2048), BF16),
         ),
-        in_specs=[vmem, vmem, hbm, hbm],
+        in_specs=[hbm] * 4,
         out_specs=(vmem, hbm, hbm, hbm, hbm),
         scratch_shapes=[
             pltpu.VMEM((NC, 2, 2, 16, 16, 512), BF16),
@@ -382,37 +389,71 @@
             pltpu.SemaphoreType.DMA((COPIES,)),
             pltpu.SemaphoreType.DMA((COPIES,)),
             pltpu.SemaphoreType.DMA((10 * NC,)),
-            pltpu.SemaphoreType.DMA((3,)),
+            pltpu.SemaphoreType.DMA((3 + 2 * NC,)),
         ],
         compiler_params=pltpu.CompilerParams(
             collective_id=0, has_side_effects=True, vmem_limit_bytes=60 * 2**20
         ),
         cost_estimate=pl.CostEstimate(flops=6 * 2**30, bytes_accessed=16 * 2**20, transcendentals=0),
     )(inputs, out_grad, w_in, w_out)
-    w_in_grad, w_out_grad = weight_grads(
-        xg.reshape(1024, 512), gg.reshape(1024, 512), act.reshape(1024, 2048), pre_grad.reshape(1024, 2048)
+    return weight_grads(
+        input_grad, xg.reshape(1024, 512), gg.reshape(1024, 512), act.reshape(1024, 2048), pre_grad.reshape(1024, 2048)
     )
-    return (input_grad, w_in_grad, w_out_grad)
-
-
-def weight_grads(xg, gg, act, pre_grad):
-    steps = 2
-    width = 2048 // steps
-    whole, columns = pl.BlockSpec((1024, 512), lambda i: (0, 0)), pl.BlockSpec((1024, width), lambda i: (0, i))
-
-    def body(x, g, a, p, w_in_grad, w_out_grad):
-        w_in_grad[...] = lax.dot_general(x[...], p[...], TN, preferred_element_type=F32)
-        w_out_grad[...] = lax.dot_general(a[...], g[...], TN, preferred_element_type=F32)
-
+
+
+def weight_grads(input_grad, xg, gg, act, pre_grad):
+    blocks = 4
+
+    def body(ig, x, g, a, p, ig_out, wi_out, wo_out, X, G, A, PG, WI, WO, isem, osem):
+        def cols(b):
+            return pl.ds(512 * b, 512)
+
+        def start(src, dst, sem):
+            copy = pltpu.make_async_copy(src, dst, sem)
+            copy.start()
+            return copy
+
+        x_in = start(x, X, isem.at[0])
+        p_in = [start(p.at[:, cols(b)], PG.at[b], isem.at[2 + b]) for b in range(blocks)]
+        g_in = start(g, G, isem.at[1])
+        a_in = [start(a.at[:, cols(b)], A.at[b], isem.at[2 + blocks + b]) for b in range(blocks)]
+        outs = [start(ig, ig_out, osem.at[2 * blocks])]
+        x_in.wait()
+        for b in range(blocks):
+            p_in[b].wait()
+            WI[b] = lax.dot_general(X[...], PG[b], TN, preferred_element_type=F32)
+            outs.append(start(WI.at[b], wi_out.at[:, cols(b)], osem.at[b]))
+        g_in.wait()
+        for b in range(blocks):
+            a_in[b].wait()
+            WO[b] = lax.dot_general(A[b], G[...], TN, preferred_element_type=F32)
+            outs.append(start(WO.at[b], wo_out.at[cols(b), :], osem.at[blocks + b]))
+        for copy in outs:
+            copy.wait()
+
+    hbm = pl.BlockSpec(memory_space=pl.ANY)
     return pl.pallas_call(
         body,
-        grid=(steps,),
-        out_shape=(jax.ShapeDtypeStruct((512, 2048), F32), jax.ShapeDtypeStruct((2048, 512), F32)),
-        in_specs=[whole, whole, columns, columns],
-        out_specs=(pl.BlockSpec((512, width), lambda i: (0, i)), pl.BlockSpec((width, 512), lambda i: (i, 0))),
+        out_shape=(
+            jax.ShapeDtypeStruct((64, 512), F32),
+            jax.ShapeDtypeStruct((512, 2048), F32),
+            jax.ShapeDtypeStruct((2048, 512), F32),
+        ),
+        in_specs=[hbm] * 5,
+        out_specs=(hbm,) * 3,
+        scratch_shapes=[
+            pltpu.VMEM((1024, 512), BF16),
+            pltpu.VMEM((1024, 512), BF16),
+            pltpu.VMEM((blocks, 1024, 512), BF16),
+            pltpu.VMEM((blocks, 1024, 512), BF16),
+            pltpu.VMEM((blocks, 512, 512), F32),
+            pltpu.VMEM((blocks, 512, 512), F32),
+            pltpu.SemaphoreType.DMA((2 + 2 * blocks,)),
+            pltpu.SemaphoreType.DMA((2 * blocks + 1,)),
+        ],
         compiler_params=pltpu.CompilerParams(vmem_limit_bytes=60 * 2**20),
         cost_estimate=pl.CostEstimate(flops=4 * 2**30, bytes_accessed=18 * 2**20, transcendentals=0),
-    )(xg, gg, act, pre_grad)
+    )(input_grad, xg, gg, act, pre_grad)
 
 
 def solution(mesh):

time: 104 us -> 102 us (0.981)
    pallas_call x1, Pallas kernels: 93.4 us -> 92.2 us  [local(): pl.pallas_call(kernel, out_shape=(jax.ShapeDtypeStruct((64, 512), F32), j...]
where the time goes in v5:
time: 102 us
  Pallas kernels  101 us (99%)
    pallas_call x1, Pallas kernels, local(): pl.pallas_call(kernel, out_shape=(jax.ShapeDtypeStruct((64, 512), F32), j...  92.2 us
    pallas_call x1, Pallas kernels, weight_grads(): pl.pallas_call(body, out_shape=(jax.ShapeDtypeStruct((64, 512), F32), jax...  8.56 us

profile of v5, /device:TPU:1, one launch (start us, length us, event | category | flops | bytes accessed | tf_op | source)
XLA Modules:
  0.0 101.5 jit_solution(12809754013511523184)
XLA Ops:
  0.6 92.2 %shard_map.67 = (f32[64,512]{1,0:T(8,128)}, bf16[4,16,16,512]{3,2,1,0:T(8,128)(2,1)}, bf16[4,16,16,512]{3,2,1,0:T(8,128)(2,1)}, bf16[4,4,2,32,2048]{4,3,2,1,0:T(8,128)(2,1)}, bf16[4,4,2,32,2048]{4,3,2,1,0:T(8,128)(2,1)}) custom-call(bf16[64,512]{1,0:T(8,128)(2,1)} %x_ref.1, bf16[64,512]{1,0:T(8,128)(2,1)} %g_ref.1, bf16[512,2048]{1,0:T(8,128)(2,1)} %w_in.1, ...), custom_call_target="tpu_custom_call" | custom-call | flops 6442450944 | bytes 16777216 | tf_op jit(solution)/shard_map/pallas_call | solution.py:362
  92.8 8.6 %shard_map.68 = (f32[64,512]{1,0:T(8,128)}, f32[512,2048]{1,0:T(8,128)}, f32[2048,512]{1,0:T(8,128)}) custom-call(f32[64,512]{1,0:T(8,128)} %get-tuple-element.8.ig, bf16[1024,512]{1,0:T(8,128)(2,1)} %bitcast.6, bf16[1024,512]{1,0:T(8,128)(2,1)} %bitcast.7, bf16[1024,2048]{1,0:T(8,128)(2,1)} %bitcast.4, bf16[1024,2048]{1,0:T(8,128)(2,1)} %bitcast.5), custom_call_target="tpu_custom_call" | custom-call | flops 4294967296 | bytes 18874368 | tf_op jit(solution)/shard_map/pallas_call | solution.py:435

commit v6 on v5

--- a/solution.py
+++ b/solution.py
@@ -17,35 +17,35 @@
 Z_FIRST = ((1, 0), (3, 1),)
 Y_FIRST = ((0, 0), (1, 0), (1, 1),)
 ORDER = (
-    ("Ax", 0, 0), ("Ag", 0, 0), ("A", 1, 0), ("A", 2, 0), ("B1x", 0, 0), ("B2x", 0, 0),
-    ("B3x", 0, 0), ("B2g", 0, 0), ("B3g", 0, 0), ("B1g", 0, 0), ("B2", 1, 0), ("B3", 1, 0),
-    ("B1", 1, 0), ("Dx", 0, 0), ("A", 3, 0), ("Ex", 0, 1), ("Dg", 0, 0), ("Ex", 0, 0),
-    ("B2", 2, 0), ("B3", 2, 0), ("Eg", 0, 0), ("Eg", 0, 1), ("D", 1, 0), ("F0x", 0, 1),
-    ("B1", 2, 0), ("F0x", 0, 0), ("B1", 3, 0), ("F1x", 0, 1), ("B2", 3, 0), ("F1x", 0, 0),
-    ("E", 1, 1), ("B3", 3, 0), ("F1g", 0, 0), ("E", 1, 0), ("F1g", 0, 1), ("D", 2, 0),
-    ("F0g", 0, 0), ("F0g", 0, 1), ("F0", 1, 1), ("F1", 1, 1), ("E", 2, 1), ("D", 3, 0),
-    ("G", 0, 0), ("E", 2, 0), ("G", 0, 1), ("E", 3, 1), ("F1", 2, 1), ("F0", 2, 1),
-    ("e", 1, 0), ("H", 0, 0), ("F1", 2, 0), ("Sp", 0, 0), ("F0", 2, 0), ("G", 1, 1),
-    ("E", 3, 0), ("F0", 1, 0), ("G", 2, 1), ("F1", 1, 0), ("e", 3, 1), ("G", 2, 0),
-    ("H", 0, 1), ("Sp", 0, 1), ("F0", 3, 0), ("F1", 3, 0), ("J1p", 0, 0), ("H", 1, 1),
-    ("J0p", 0, 0), ("Sa", 0, 1), ("Sp", 1, 1), ("H", 2, 1), ("H", 1, 0), ("Sp", 1, 0),
-    ("Sp", 2, 1), ("H", 2, 0), ("Sp", 2, 0), ("F0", 3, 1), ("Sa", 1, 1), ("Sa", 2, 1),
-    ("F1", 3, 1), ("Ip", 0, 1), ("G", 3, 0), ("kp", 0, 0), ("J1p", 1, 0), ("J0p", 1, 0),
-    ("J1p", 1, 1), ("Ip", 2, 1), ("H", 3, 1), ("J0p", 1, 1), ("Sp", 3, 1), ("Sa", 1, 0),
-    ("H", 3, 0), ("Sp", 3, 0), ("J0p", 0, 1), ("Ip", 2, 0), ("J0a", 1, 1), ("J1a", 1, 1),
-    ("kp", 1, 0), ("J1p", 0, 1), ("kp", 1, 1), ("Kp", 0, 0), ("Sa", 0, 0), ("J0p", 2, 1),
-    ("J1a", 1, 0), ("J0a", 1, 0), ("Sa", 3, 1), ("Sa", 3, 0), ("Sa", 2, 0), ("Ip", 3, 0),
-    ("Ip", 3, 1), ("ka", 1, 1), ("J1p", 2, 0), ("Kp", 0, 1), ("J0p", 2, 0), ("L", 0, 0),
-    ("J1p", 2, 1), ("Kp", 1, 0), ("J0a", 0, 0), ("Ia", 0, 1), ("L", 0, 1), ("J1p", 3, 0),
-    ("J1a", 0, 0), ("J0p", 3, 0), ("Kp", 1, 1), ("L", 1, 0), ("J1p", 3, 1), ("J0p", 3, 1),
-    ("Kp", 2, 1), ("Kp", 2, 0), ("L", 1, 1), ("Ia", 3, 0), ("Ia", 2, 0), ("ka", 1, 0),
-    ("L", 2, 0), ("Kp", 3, 0), ("L", 2, 1), ("Kp", 3, 1), ("ka", 0, 0), ("Ia", 2, 1),
-    ("L", 3, 0), ("Ia", 3, 1), ("L", 3, 1), ("N", 1, 1), ("N", 0, 1), ("Ka", 1, 1),
-    ("J0a", 0, 1), ("J1a", 3, 0), ("J1a", 2, 1), ("J1a", 2, 0), ("J0a", 2, 0), ("J0a", 2, 1),
-    ("N", 2, 1), ("Ka", 0, 0), ("J0a", 3, 1), ("J1a", 0, 1), ("J0a", 3, 0), ("J1a", 3, 1),
-    ("N", 3, 1), ("Ka", 1, 0), ("Ka", 2, 0), ("Ka", 2, 1), ("O", 0, 1), ("Ka", 0, 1),
-    ("Ka", 3, 0), ("Q", 1, 0), ("Ka", 3, 1), ("Q", 2, 1), ("O", 2, 1), ("Q", 0, 0),
-    ("Q", 1, 1), ("Q", 0, 1), ("O", 1, 1), ("Q", 2, 0), ("Q", 3, 0), ("Q", 3, 1),
+    ("Ax", 0, 0), ("Ag", 0, 0), ("A", 1, 0), ("A", 2, 0), ("B1x", 0, 0), ("B3x", 0, 0),
+    ("B2x", 0, 0), ("B1g", 0, 0), ("B3g", 0, 0), ("B2g", 0, 0), ("B2", 1, 0), ("B3", 1, 0),
+    ("Dx", 0, 0), ("B1", 1, 0), ("A", 3, 0), ("Ex", 0, 1), ("Dg", 0, 0), ("Ex", 0, 0),
+    ("B3", 2, 0), ("B1", 2, 0), ("Eg", 0, 0), ("B2", 2, 0), ("D", 1, 0), ("F0x", 0, 1),
+    ("F1x", 0, 1), ("Eg", 0, 1), ("F1x", 0, 0), ("B1", 3, 0), ("F0x", 0, 0), ("E", 1, 1),
+    ("B2", 3, 0), ("E", 1, 0), ("F1g", 0, 0), ("D", 2, 0), ("F1g", 0, 1), ("F0g", 0, 1),
+    ("B3", 3, 0), ("F0g", 0, 0), ("F1", 1, 1), ("F0", 1, 1), ("E", 2, 1), ("E", 2, 0),
+    ("G", 0, 1), ("G", 0, 0), ("D", 3, 0), ("F0", 2, 1), ("G", 1, 1), ("F1", 2, 1),
+    ("E", 3, 1), ("E", 3, 0), ("F0", 2, 0), ("F1", 2, 0), ("e", 1, 0), ("H", 1, 1),
+    ("H", 0, 0), ("H", 0, 1), ("G", 2, 1), ("Sp", 0, 0), ("F1", 3, 0), ("F0", 3, 0),
+    ("Sp", 0, 1), ("G", 2, 0), ("F0", 1, 0), ("Sa", 0, 1), ("F1", 1, 0), ("e", 3, 1),
+    ("Sp", 1, 1), ("J0p", 0, 0), ("J1p", 0, 0), ("H", 2, 1), ("Sp", 2, 1), ("Ip", 0, 1),
+    ("G", 3, 0), ("H", 2, 0), ("Sp", 2, 0), ("F0", 3, 1), ("Sa", 0, 0), ("H", 1, 0),
+    ("Sa", 2, 1), ("F1", 3, 1), ("Sp", 1, 0), ("J1p", 1, 1), ("kp", 0, 0), ("J0p", 1, 1),
+    ("Sa", 1, 0), ("Ip", 2, 0), ("H", 3, 0), ("J1p", 0, 1), ("Sp", 3, 0), ("J0p", 0, 1),
+    ("H", 3, 1), ("J0p", 1, 0), ("J1p", 1, 0), ("Sp", 3, 1), ("Ip", 2, 1), ("kp", 1, 1),
+    ("Kp", 0, 0), ("Sa", 1, 1), ("Ip", 3, 0), ("J0p", 2, 0), ("J1p", 2, 0), ("J0a", 0, 0),
+    ("J1a", 0, 0), ("kp", 1, 0), ("Kp", 0, 1), ("L", 0, 0), ("J0p", 2, 1), ("J1p", 2, 1),
+    ("Ip", 3, 1), ("Sa", 3, 1), ("L", 0, 1), ("Kp", 1, 1), ("Sa", 2, 0), ("J0p", 3, 0),
+    ("Sa", 3, 0), ("J1a", 1, 0), ("J1a", 1, 1), ("Kp", 2, 0), ("J0a", 1, 0), ("J1p", 3, 0),
+    ("Ia", 0, 1), ("J0a", 1, 1), ("Kp", 2, 1), ("ka", 0, 0), ("L", 2, 0), ("Kp", 1, 0),
+    ("J1p", 3, 1), ("J0p", 3, 1), ("L", 2, 1), ("Ia", 2, 1), ("Ia", 3, 1), ("ka", 1, 0),
+    ("L", 1, 0), ("Kp", 3, 0), ("L", 1, 1), ("Kp", 3, 1), ("Ia", 3, 0), ("ka", 1, 1),
+    ("Ia", 2, 0), ("J1a", 0, 1), ("L", 3, 0), ("L", 3, 1), ("J0a", 0, 1), ("N", 0, 1),
+    ("J0a", 3, 1), ("J1a", 3, 1), ("Ka", 1, 0), ("J1a", 2, 1), ("N", 2, 1), ("Ka", 0, 0),
+    ("J0a", 3, 0), ("J0a", 2, 1), ("J1a", 3, 0), ("J1a", 2, 0), ("N", 1, 1), ("J0a", 2, 0),
+    ("Ka", 1, 1), ("Q", 1, 0), ("Ka", 3, 1), ("N", 3, 1), ("Ka", 3, 0), ("Ka", 2, 0),
+    ("Ka", 2, 1), ("Q", 0, 0), ("Q", 1, 1), ("Ka", 0, 1), ("Q", 3, 1), ("Q", 2, 0),
+    ("O", 2, 1), ("Q", 0, 1), ("Q", 3, 0), ("Q", 2, 1), ("O", 1, 1), ("O", 0, 1),
     ("O", 3, 1),
 )
 
@@ -291,7 +291,7 @@
     def whole(a, c, u):
         arrived(("K", a, c, u))
         for half in range(2):
-            keep(ACT.at[c, a, half, u], (ao, po)[a].at[c, :, :, :, pl.ds(1024 * half + 512 * u, 512)])
+            keep(ACT.at[c, a, half, u], (ao, po)[a].at[2 * half + u, c])
 
     def L(c, u):
         whole(1, c, u)
@@ -365,8 +365,8 @@
             jax.ShapeDtypeStruct((64, 512), F32),
             jax.ShapeDtypeStruct((NC, 16, 16, 512), BF16),
             jax.ShapeDtypeStruct((NC, 16, 16, 512), BF16),
-            jax.ShapeDtypeStruct((NC, 4, 2, 32, 2048), BF16),
-            jax.ShapeDtypeStruct((NC, 4, 2, 32, 2048), BF16),
+            jax.ShapeDtypeStruct((2 * Q, NC, 4, 2, 32, 512), BF16),
+            jax.ShapeDtypeStruct((2 * Q, NC, 4, 2, 32, 512), BF16),
         ),
         in_specs=[hbm] * 4,
         out_specs=(vmem, hbm, hbm, hbm, hbm),
@@ -397,7 +397,7 @@
         cost_estimate=pl.CostEstimate(flops=6 * 2**30, bytes_accessed=16 * 2**20, transcendentals=0),
     )(inputs, out_grad, w_in, w_out)
     return weight_grads(
-        input_grad, xg.reshape(1024, 512), gg.reshape(1024, 512), act.reshape(1024, 2048), pre_grad.reshape(1024, 2048)
+        input_grad, xg.reshape(1024, 512), gg.reshape(1024, 512), act.reshape(4, 1024, 512), pre_grad.reshape(4, 1024, 512)
     )
 
 
@@ -414,9 +414,9 @@
             return copy
 
         x_in = start(x, X, isem.at[0])
-        p_in = [start(p.at[:, cols(b)], PG.at[b], isem.at[2 + b]) for b in range(blocks)]
+        p_in = [start(p.at[b], PG.at[b], isem.at[2 + b]) for b in range(blocks)]
         g_in = start(g, G, isem.at[1])
-        a_in = [start(a.at[:, cols(b)], A.at[b], isem.at[2 + blocks + b]) for b in range(blocks)]
+        a_in = [start(a.at[b], A.at[b], isem.at[2 + blocks + b]) for b in range(blocks)]
         outs = [start(ig, ig_out, osem.at[2 * blocks])]
         x_in.wait()
         for b in range(blocks):

time: 102 us -> 102 us (level)
  no operation moved by 1% of the time
where the time goes in v6:
time: 102 us
  Pallas kernels  101 us (99%)
    pallas_call x1, Pallas kernels, local(): pl.pallas_call(kernel, out_shape=(jax.ShapeDtypeStruct((64, 512), F32), j...  92.3 us
    pallas_call x1, Pallas kernels, weight_grads(): pl.pallas_call(body, out_shape=(jax.ShapeDtypeStruct((64, 512), F32), jax...  8.56 us

profile of v6, /device:TPU:1, one launch (start us, length us, event | category | flops | bytes accessed | tf_op | source)
XLA Modules:
  0.0 101.6 jit_solution(10914703722474453893)
XLA Ops:
  0.6 92.3 %shard_map.67 = (f32[64,512]{1,0:T(8,128)}, bf16[4,16,16,512]{3,2,1,0:T(8,128)(2,1)}, bf16[4,16,16,512]{3,2,1,0:T(8,128)(2,1)}, bf16[4,4,4,2,32,512]{5,4,3,2,1,0:T(8,128)(2,1)}, bf16[4,4,4,2,32,512]{5,4,3,2,1,0:T(8,128)(2,1)}) custom-call(bf16[64,512]{1,0:T(8,128)(2,1)} %x_ref.1, bf16[64,512]{1,0:T(8,128)(2,1)} %g_ref.1, bf16[512,2048]{1,0:T(8,128)(2,1)} %w_in.1, ...), custom_call_target="tpu_custom_call" | custom-call | flops 6442450944 | bytes 16777216 | tf_op jit(solution)/shard_map/pallas_call | solution.py:362
  92.9 8.6 %shard_map.68 = (f32[64,512]{1,0:T(8,128)}, f32[512,2048]{1,0:T(8,128)}, f32[2048,512]{1,0:T(8,128)}) custom-call(f32[64,512]{1,0:T(8,128)} %get-tuple-element.8.ig, bf16[1024,512]{1,0:T(8,128)(2,1)} %bitcast.6, bf16[1024,512]{1,0:T(8,128)(2,1)} %bitcast.7, bf16[4,1024,512]{2,1,0:T(8,128)(2,1)} %bitcast.4, bf16[4,1024,512]{2,1,0:T(8,128)(2,1)} %bitcast.5), custom_call_target="tpu_custom_call" | custom-call | flops 4294967296 | bytes 18874368 | tf_op jit(solution)/shard_map/pallas_call | solution.py:435
